TPU v7x, 128 devices: a whole 4x4x4 slice. The times are simulated.
128 devices in a mesh: rep: 32 (over x, z, core), tp: 4 (over y).
Axes of the slice: x: 4, y: 4, z: 4, core: 2. Of those that a mesh axis runs over, the one named last changes fastest.
Arguments:
- query: bfloat16 [1024, 4096], P('rep', 'tp'), may hold values from -8 to 8
- kv_pool: bfloat16 [2, 4, 8192, 64, 128], P(None, 'tp', 'rep'), may hold values from -6 to 6
- page_table: int32 [1024, 8], P('rep'), may hold values from 0 to 255, as said below
- lengths: int32 [1024], P('rep'), may hold values from 1 to 512, 262144 in all
- residual: bfloat16 [1024, 4096], P('rep'), may hold values from -64 to 64
- w_out: bfloat16 [4096, 4096], P('tp'), may hold values from -0.09375 to 0.09375
- norm_gain: bfloat16 [4096], replicated, may hold values from 0.099609375 to 1.8984375
- route_ids: int32 [1024, 8], P('rep'), may hold values from 0 to 31, all different within a row; in each aligned block of 32 rows (0 to 31, 32 to 63, ...) at most 16 rows name the same one
- route_weights: float32 [1024, 8], P('rep'), may hold values from 0.05 to 1
- w_gate: bfloat16 [32, 4096, 1536], P('rep', None, 'tp'), may hold values from -0.09375 to 0.09375
- w_up: bfloat16 [32, 4096, 1536], P('rep', None, 'tp'), may hold values from -0.09375 to 0.09375
- w_down: bfloat16 [32, 1536, 4096], P('rep', 'tp'), may hold values from -0.15625 to 0.15625
Outputs:
- layer_out: bfloat16 [1024, 4096], P('rep', 'tp')
Inputs may be any that keep to these rules, and one draw needn't show every extreme that they name: `page_table`: each replica's 32 rows hold distinct pages of that replica's pool, and together all of them. `route_ids`: within the 32 rows of one replica no expert is named by more than 16 rows; a row names 8 different experts.
All inputs are finite; a program needn't handle non-finite values. No bound on the sum of `lengths` on one device may be relied on, other than what follows from the above.
Results may differ from a plain program's by a relative error of at most 0.0035.
Values may be sent and summed in bfloat16 or wider, within the bound.
A program may use at most 128 MiB of HBM per device.

v0:
```python
import jax
import jax.numpy as jnp
from jax import lax
from jax.sharding import PartitionSpec as P

norm_epsilon = 1e-06


def local(
    query,
    kv_pool,
    page_table,
    lengths,
    residual,
    w_out,
    norm_gain,
    route_ids,
    route_weights,
    w_gate,
    w_up,
    w_down,
):
    row_count = query.shape[0]
    kv_local = kv_pool.shape[1]
    page_len = kv_pool.shape[3]
    head_dim = kv_pool.shape[4]
    group_size = query.shape[1] // (kv_local * head_dim)
    context = page_table.shape[1] * page_len
    feature_count = residual.shape[1]
    share_width = feature_count // lax.axis_size("tp")
    tp_pos = lax.axis_index("tp")
    owner_count = lax.axis_size("rep")
    top_count = route_ids.shape[1]
    capacity = min(row_count, 2 * row_count * top_count // owner_count)
    slot_total = owner_count * capacity
    cache = jnp.take(kv_pool, page_table.reshape(-1), axis=2)
    cache = cache.reshape(2, kv_local, row_count, context, head_dim)
    queries = query.reshape(row_count, kv_local, group_size, head_dim)
    scores = jnp.einsum("rkgd,krcd->rkgc", queries, cache[0], preferred_element_type=jnp.float32)
    scores = scores * head_dim ** (-0.5)
    valid_keys = jnp.arange(context, dtype=jnp.int32)[None, :] < lengths[:, None]
    scores = jnp.where(valid_keys[:, None, None, :], scores, -1e30)
    top_score = jnp.max(scores, axis=-1, keepdims=True)
    weights = jnp.exp(scores - top_score)
    probs = (weights / jnp.sum(weights, axis=-1, keepdims=True)).astype(jnp.bfloat16)
    mixed = jnp.einsum("rkgc,krcd->rkgd", probs, cache[1], preferred_element_type=jnp.float32)
    attn = mixed.reshape(row_count, kv_local * group_size * head_dim).astype(jnp.bfloat16)
    partial_out = jnp.dot(attn, w_out, preferred_element_type=jnp.float32)
    flat_ids = route_ids.reshape(-1)
    expert_iota = jnp.arange(owner_count, dtype=jnp.int32)
    onehot = (flat_ids[:, None] == expert_iota[None, :]).astype(jnp.int32)
    slot_index = jnp.sum((jnp.cumsum(onehot, axis=0) - onehot) * onehot, axis=1)
    target = flat_ids * capacity + slot_index
    slot_iota = jnp.arange(slot_total, dtype=jnp.int32)
    hits = (target[:, None] == slot_iota[None, :]).reshape(row_count, top_count, slot_total)
    select_rows = jnp.any(hits, axis=1).astype(jnp.bfloat16)
    combine = jnp.sum(hits.astype(jnp.float32) * route_weights[:, :, None], axis=1)
    attn_sum = lax.psum(partial_out, "tp")
    hidden = residual.astype(jnp.float32) + attn_sum
    mean_square = jnp.mean(hidden * hidden, axis=-1, keepdims=True)
    normed = (
        hidden * lax.rsqrt(mean_square + norm_epsilon) * norm_gain.astype(jnp.float32)
    ).astype(jnp.bfloat16)
    hidden_share = lax.dynamic_slice_in_dim(hidden, tp_pos * share_width, share_width, 1)
    outgoing = jnp.einsum("rs,rd->sd", select_rows, normed, preferred_element_type=jnp.float32)
    outgoing = outgoing.astype(jnp.bfloat16).reshape(owner_count, capacity, feature_count)
    arrived = lax.all_to_all(outgoing, "rep", split_axis=0, concat_axis=0, tiled=True).reshape(
        slot_total, feature_count
    )
    gate = jnp.dot(arrived, w_gate[0], preferred_element_type=jnp.float32)
    upward = jnp.dot(arrived, w_up[0], preferred_element_type=jnp.float32)
    act = (jax.nn.silu(gate) * upward).astype(jnp.bfloat16)
    expert_terms = jnp.dot(act, w_down[0], preferred_element_type=jnp.float32)
    summed = lax.psum_scatter(expert_terms, "tp", scatter_dimension=1, tiled=True).astype(
        jnp.bfloat16
    )
    results = lax.all_to_all(
        summed.reshape(owner_count, capacity, share_width),
        "rep",
        split_axis=0,
        concat_axis=0,
        tiled=True,
    )
    moe = jnp.dot(
        combine,
        results.reshape(slot_total, share_width).astype(jnp.float32),
        precision=lax.Precision.HIGHEST,
    )
    return (hidden_share + moe).astype(jnp.bfloat16)


def solution(mesh):
    in_specs = (
        P("rep", "tp"),
        P(None, "tp", "rep", None, None),
        P("rep", None),
        P("rep"),
        P("rep", None),
        P("tp", None),
        P(),
        P("rep", None),
        P("rep", None),
        P("rep", None, "tp"),
        P("rep", None, "tp"),
        P("rep", "tp", None),
    )
    out_specs = P("rep", "tp")
    return jax.shard_map(local, mesh=mesh, in_specs=in_specs, out_specs=out_specs, check_vma=False)
```

profile of v0, /device:TPU:1, one launch (start us, length us, event | category | flops | bytes accessed | tf_op | source)
XLA Modules:
  0.0 282.3 jit_solution(11292648466958437164)
XLA Ops:
  6.5 0.9 copy.22
  7.7 12.0 %gather_fusion = bf16[256,2,64,128]{3,2,1,0:T(8,128)(2,1)} fusion(bf16[2,256,64,128]{3,2,1,0:T(8,128)(2,1)} %bitcast.68, s32[1024]{0:T(1024)S(1)} %pad_clamp_fusion), kind=kCustom, calls=%fused_computation | custom fusion | bytes 16778240 | tf_op jit(solution)/shard_map/jit(_take)/gather | solution.py:36
  19.7 7.4 %bitcast_select_fusion = bf16[2,1,256,64,128]{4,3,0,2,1:T(8,128)(2,1)} fusion(bf16[256,2,64,128]{3,2,1,0:T(8,128)(2,1)} %gather_fusion, pred[256]{0:T(512)(128)(4,1)S(1)} %compare_and_fusion), kind=kLoop, calls=%fused_computation.2 | loop fusion | flops 4194304 | bytes 16777472 | tf_op jit(solution)/shard_map/jit(_take)/select_n | solution.py:36
  27.1 5.8 %fusion.38 = (bf16[1,1,256,64,128]{4,3,0,2,1:T(8,128)(2,1)S(1)}, bf16[1,1,256,64,128]{4,3,0,2,1:T(8,128)(2,1)}) fusion(bf16[2,1,256,64,128]{4,3,0,2,1:T(8,128)(2,1)} %bitcast_select_fusion), kind=kLoop, calls=%fused_computation.56 | loop fusion | bytes 16777216 | tf_op jit(solution)/shard_map/slice | solution.py:39
  33.1 1.2 fusion.16
  34.3 0.8 copy-done.1
  35.1 0.2 fusion.39
  35.3 3.2 %convolution_convert_fusion.1 = bf16[32,8,128]{2,1,0:T(8,128)(2,1)S(1)} fusion(bf16[32,512,128]{2,1,0:T(8,128)(2,1)} %bitcast.66, f32[32,8]{1,0:T(8,128)S(1)} %fusion.39, f32[32,8,512]{2,1,0:T(8,128)} %copy-done.1), kind=kOutput, calls=%fused_computation.19 | convolution fusion | flops 33981184 | bytes 4785152 | tf_op jit(solution)/shard_map/rkgc,krcd->rkgd/dot_general | solution.py:46
  38.6 5.8 %fusion.30 = f32[32,4096]{1,0:T(8,128)} fusion(bf16[1024,4096]{1,0:T(8,128)(2,1)} %param.17, bf16[4,8,8,128]{3,2,1,0:T(8,128)(2,1)S(1)} %bitcast.72), kind=kOutput, calls=%fused_computation.36 | convolution fusion | flops 268435456 | bytes 8978432 | tf_op jit(solution)/shard_map/dot_general | solution.py:48
  44.7 0.6 reduce-window.6
  45.8 0.2 fusion.25
  46.0 42.8 %all-reduce.2.cloned.1.call-done = f32[32,4096]{1,0:T(8,128)} async-done(((f32[32,4096]{1,0:T(8,128)}), f32[32,4096]{1,0:T(8,128)}) %all-reduce.2.cloned.1.call-update) | async-done | bytes 524304 | tf_op jit(solution)/shard_map/psum | solution.py:58
  88.7 1.2 multiply_reduce_fusion
  90.0 1.3 convolution_convert_fusion
  91.3 60.3 %all_to_all.10 = bf16[32,16,4096]{2,1,0:T(8,128)(2,1)S(1)} all-to-all(bf16[32,16,4096]{2,1,0:T(8,128)(2,1)S(1)} %bitcast.65), channel_id=1, replica_groups=mesh['rep'=32,'tp'=4] {'rep'}, dimensions={0} | all-to-all | bytes 8388608 | tf_op jit(solution)/shard_map/all_to_all | solution.py:67
  151.7 2.0 copy-done.2
  153.7 3.3 %fusion.5 = f32[512,384]{1,0:T(8,128)} fusion(bf16[512,4096]{1,0:T(8,128)(2,1)S(1)} %bitcast.70, bf16[1,4096,384]{2,1,0:T(8,128)(2,1)S(1)} %copy-done.10), kind=kOutput, calls=%fused_computation.8 | convolution fusion | flops 1610612736 | bytes 8126464 | tf_op jit(solution)/shard_map/dot_general | solution.py:70
  157.0 11.0 %fusion.1 = f32[512,4096]{1,0:T(8,128)} fusion(bf16[1,384,4096]{2,1,0:T(8,128)(2,1)S(1)} %copy-done, bf16[512,4096]{1,0:T(8,128)(2,1)} %bitcast.71, bf16[1,4096,384]{2,1,0:T(8,128)(2,1)} %param.22, f32[512,384]{1,0:T(8,128)} %fusion.5), kind=kOutput, calls=%fused_computation.4 | convolution fusion | flops 3222405120 | bytes 19660800 | tf_op jit(solution)/shard_map/dot_general | solution.py:73
  168.0 77.6 %reduce-scatter.2.cloned.1.call-done = f32[512,1024]{1,0:T(8,128)} async-done(((f32[512,4096]{1,0:T(8,128)}), f32[512,1024]{1,0:T(8,128)}) %reduce-scatter.2.cloned.1.call-update) | async-done | bytes 2097168 | tf_op jit(solution)/shard_map/reduce_scatter | solution.py:74
  245.6 2.8 convert_element_type.51
  248.4 7.7 %all-to-all-start.1 = ((bf16[32,16,1024]{2,1,0:T(8,128)(2,1)}), bf16[32,16,1024]{2,1,0:T(8,128)(2,1)}, u32[]{:S(2)}, u32[]{:S(2)}) async-start(bf16[32,16,1024]{2,1,0:T(8,128)(2,1)} %bitcast.69), calls=%async_computation.2 | async-start | bytes 2097152 | tf_op jit(solution)/shard_map/all_to_all | solution.py:77
  256.2 0.2 select_reduce_fusion
  256.4 16.6 %all-to-all-done.1 = bf16[32,16,1024]{2,1,0:T(8,128)(2,1)} async-done(((bf16[32,16,1024]{2,1,0:T(8,128)(2,1)}), bf16[32,16,1024]{2,1,0:T(8,128)(2,1)}, u32[]{:S(2)}, u32[]{:S(2)}) %all-to-all-start.1) | async-done | bytes 1048608 | tf_op jit(solution)/shard_map/all_to_all | solution.py:77
  273.0 2.5 fusion.19
  (44 shorter events, 1.2 us)
Async XLA Ops:
  6.5 150.4 %copy-start = (bf16[1,384,4096]{2,1,0:T(8,128)(2,1)S(1)}, bf16[1,384,4096]{2,1,0:T(8,128)(2,1)}, u32[]{:S(2)}) copy-start(bf16[1,384,4096]{2,1,0:T(8,128)(2,1)} %param.23) | copy-start | bytes 9437188
  6.5 82.2 %all-reduce.2.cloned.1.call-start = ((), (), s32[]{:S(2)}) async-start(), calls=%async_computation.3 | async-start | bytes 1048576 | tf_op jit(solution)/shard_map/psum | solution.py:58
  27.1 5.9 %copy-start.5 = (bf16[32,1024]{1,0:T(8,128)(2,1)S(1)}, bf16[32,1024]{1,0:T(8,128)(2,1)}, u32[]{:S(2)}) copy-start(bf16[32,1024]{1,0:T(8,128)(2,1)} %param.12) | copy-start | bytes 196612
  27.1 5.9 %copy-start.9 = (s32[32]{0:T(128)S(1)}, s32[32]{0:T(128)}, u32[]{:S(2)}) copy-start(s32[32]{0:T(128)} %param.15) | copy-start | bytes 388
  34.3 0.8 copy-start.1
  38.5 5.9 %copy-start.7 = (s32[32,8]{0,1:T(8,128)S(1)}, s32[32,8]{0,1:T(8,128)}, u32[]{:S(2)}) copy-start(s32[32,8]{0,1:T(8,128)} %param.19) | copy-start | bytes 3076
  38.5 7.2 %copy-start.6 = (bf16[4096]{0:T(1024)(128)(2,1)S(1)}, bf16[4096]{0:T(1024)(128)(2,1)}, u32[]{:S(2)}) copy-start(bf16[4096]{0:T(1024)(128)(2,1)} %param.18) | copy-start | bytes 24580
  38.6 50.2 %copy-start.4 = (bf16[32,4096]{1,0:T(8,128)(2,1)S(1)}, bf16[32,4096]{1,0:T(8,128)(2,1)}, u32[]{:S(2)}) copy-start(bf16[32,4096]{1,0:T(8,128)(2,1)} %param.16) | copy-start | bytes 786436
  44.4 201.2 %reduce-scatter.2.cloned.1.call-start = ((), (), s32[]{:S(2)}) async-start(), calls=%async_computation.4 | async-start | bytes 10485760 | tf_op jit(solution)/shard_map/reduce_scatter | solution.py:74
  90.0 1.3 copy-start.3
  91.3 62.3 %copy-start.10 = (bf16[1,4096,384]{2,1,0:T(8,128)(2,1)S(1)}, bf16[1,4096,384]{2,1,0:T(8,128)(2,1)}, u32[]{:S(2)}) copy-start(bf16[1,4096,384]{2,1,0:T(8,128)(2,1)} %param.21) | copy-start | bytes 9437188
  151.7 2.0 copy-start.2
  168.0 88.1 %copy-start.8 = (f32[32,8]{0,1:T(8,128)S(1)}, f32[32,8]{0,1:T(8,128)}, u32[]{:S(2)}) copy-start(f32[32,8]{0,1:T(8,128)} %param.20) | copy-start | bytes 3076
  248.4 24.6 %all-to-all-start.1 = ((bf16[32,16,1024]{2,1,0:T(8,128)(2,1)}), bf16[32,16,1024]{2,1,0:T(8,128)(2,1)}, u32[]{:S(2)}, u32[]{:S(2)}) async-start(bf16[32,16,1024]{2,1,0:T(8,128)(2,1)} %bitcast.69), calls=%async_computation.2 | async-start | bytes 2097152 | tf_op jit(solution)/shard_map/all_to_all | solution.py:77
Sparse Core Ops, SparseCore 0:
  44.5 44.2 all-reduce.1
  168.1 77.4 reduce-scatter.1
where the time goes:
time: 283 us; the launch traced here: 282 us
  waiting for transfers between devices  137 us (48%)
  blocking collectives  60.3 us (21%)
  matrix products  28.3 us (10%)
  local copies, waits for them, and re-layouts  22.4 us (8%)
  between operations  13.6 us (5%)
  other arithmetic  13 us (5%)
  starting transfers between devices  7.7 us (3%)
    reduce_scatter x1, waiting for transfers between devices, local(): lax.psum_scatter(expert_terms, 'tp', scatter_dimension=1, tiled=True)  77.6 us
    all_to_all x1, blocking collectives, local(): lax.all_to_all(outgoing, 'rep', split_axis=0, concat_axis=0, tiled=True)  60.3 us
    psum x1, waiting for transfers between devices, local(): attn_sum = lax.psum(partial_out, 'tp')  42.8 us
    all_to_all x1, waiting for transfers between devices, local(): lax.all_to_all(summed.reshape(owner_count, capacity, share_width), 'rep',...  16.6 us
    gather x1, local copies, waits for them, and re-layouts, local(): cache = jnp.take(kv_pool, page_table.reshape(-1), axis=2)  12 us
    dot_general x1, matrix products, local(): expert_terms = jnp.dot(act, w_down[0], preferred_element_type=jnp.float32)  11 us
    all_to_all x1, starting transfers between devices, local(): lax.all_to_all(summed.reshape(owner_count, capacity, share_width), 'rep',...  7.66 us
    select_n x2, other arithmetic, local(): cache = jnp.take(kv_pool, page_table.reshape(-1), axis=2)  7.45 us
  transfers between devices with their start and end apart: 3, of which 3 were waited for; matrix products, arithmetic and copies ran while one was open for 1% of the time, Pallas kernels for 0%

commit v1 on v0

v1 whole, which is shorter than its diff:
```python
import jax
import jax.numpy as jnp
from jax import lax
from jax.sharding import PartitionSpec as P

norm_epsilon = 1e-06


def local(
    query,
    kv_pool,
    page_table,
    lengths,
    residual,
    w_out,
    norm_gain,
    route_ids,
    route_weights,
    w_gate,
    w_up,
    w_down,
):
    row_count = query.shape[0]
    kv_local = kv_pool.shape[1]
    page_len = kv_pool.shape[3]
    head_dim = kv_pool.shape[4]
    group_size = query.shape[1] // (kv_local * head_dim)
    context = page_table.shape[1] * page_len
    feature_count = residual.shape[1]
    share_width = feature_count // lax.axis_size("tp")
    tp_pos = lax.axis_index("tp")
    rep_pos = lax.axis_index("rep")
    owner_count = lax.axis_size("rep")
    top_count = route_ids.shape[1]
    expert_iota = jnp.arange(owner_count, dtype=jnp.int32)
    onehot = route_ids[:, :, None] == expert_iota[None, None, :]
    spread = jnp.sum(jnp.where(onehot, route_weights[:, :, None], 0.0), axis=1)
    spread_all = lax.all_gather(spread, "rep", axis=0, tiled=True)
    own_weight = lax.dynamic_slice_in_dim(spread_all, rep_pos, 1, 1)

    cache = jnp.take(kv_pool, page_table.reshape(-1), axis=2)
    cache = cache.reshape(2, kv_local, row_count, context, head_dim)
    queries = query.reshape(row_count, kv_local, group_size, head_dim)
    scores = jnp.einsum("rkgd,krcd->rkgc", queries, cache[0], preferred_element_type=jnp.float32)
    scores = scores * head_dim ** (-0.5)
    valid_keys = jnp.arange(context, dtype=jnp.int32)[None, :] < lengths[:, None]
    scores = jnp.where(valid_keys[:, None, None, :], scores, -1e30)
    top_score = jnp.max(scores, axis=-1, keepdims=True)
    weights = jnp.exp(scores - top_score)
    probs = (weights / jnp.sum(weights, axis=-1, keepdims=True)).astype(jnp.bfloat16)
    mixed = jnp.einsum("rkgc,krcd->rkgd", probs, cache[1], preferred_element_type=jnp.float32)
    attn = mixed.reshape(row_count, kv_local * group_size * head_dim).astype(jnp.bfloat16)
    partial_out = jnp.dot(attn, w_out, preferred_element_type=jnp.float32)
    attn_share = lax.psum_scatter(partial_out, "tp", scatter_dimension=1, tiled=True)
    residual_share = lax.dynamic_slice_in_dim(residual, tp_pos * share_width, share_width, 1)
    gain_share = lax.dynamic_slice_in_dim(norm_gain, tp_pos * share_width, share_width, 0)
    hidden = residual_share.astype(jnp.float32) + attn_share
    square_sum = lax.psum(jnp.sum(hidden * hidden, axis=-1, keepdims=True), "tp")
    mean_square = square_sum / feature_count
    normed = (
        hidden * lax.rsqrt(mean_square + norm_epsilon) * gain_share.astype(jnp.float32)
    ).astype(jnp.bfloat16)
    rows = lax.all_gather(normed, "tp", axis=1, tiled=True)
    rows = lax.all_gather(rows, "rep", axis=0, tiled=True)
    gate = jnp.dot(rows, w_gate[0], preferred_element_type=jnp.float32)
    upward = jnp.dot(rows, w_up[0], preferred_element_type=jnp.float32)
    act = (jax.nn.silu(gate) * upward).astype(jnp.bfloat16)
    expert_terms = jnp.dot(act, w_down[0], preferred_element_type=jnp.float32)
    expert_terms = (expert_terms * own_weight).astype(jnp.bfloat16)
    moe = lax.psum_scatter(expert_terms, "tp", scatter_dimension=1, tiled=True)
    moe = lax.psum_scatter(moe, "rep", scatter_dimension=0, tiled=True)
    return (hidden + moe.astype(jnp.float32)).astype(jnp.bfloat16)


def solution(mesh):
    in_specs = (
        P("rep", "tp"),
        P(None, "tp", "rep", None, None),
        P("rep", None),
        P("rep"),
        P("rep", None),
        P("tp", None),
        P(),
        P("rep", None),
        P("rep", None),
        P("rep", None, "tp"),
        P("rep", None, "tp"),
        P("rep", "tp", None),
    )
    out_specs = P("rep", "tp")
    return jax.shard_map(local, mesh=mesh, in_specs=in_specs, out_specs=out_specs, check_vma=False)
```

time: 283 us -> 335 us (1.18)
  waiting for transfers between devices: 137 us -> 209 us
  blocking collectives: 60.3 us -> 49 us
  starting transfers between devices: 7.7 us -> 0.13 us
    reduce_scatter x1 -> x3, waiting for transfers between devices: 77.6 us -> 183 us  [the longest x1 80.5 us: local(): moe = lax.psum_scatter(moe, 'rep', scatter_dimension=0, tiled=True)]
    all_to_all x1 -> x0, blocking collectives: 60.3 us -> none  [local(): lax.all_to_all(outgoing, 'rep', split_axis=0, concat_axis=0, tiled=True)]
    psum x1 -> x0, waiting for transfers between devices: 42.8 us -> none  [local(): attn_sum = lax.psum(partial_out, 'tp')]
    all_gather x0 -> x2, blocking collectives: none -> 42.4 us  [the longest x1 32.3 us: local(): spread_all = lax.all_gather(spread, 'rep', axis=0, tiled=True)]
    all_gather x0 -> x1, waiting for transfers between devices: none -> 26.8 us  [local(): rows = lax.all_gather(rows, 'rep', axis=0, tiled=True)]
    all_to_all x1 -> x0, waiting for transfers between devices: 16.6 us -> none  [local(): lax.all_to_all(summed.reshape(owner_count, capacity, share_width), 'rep',...]
    all_to_all x1 -> x0, starting transfers between devices: 7.66 us -> none  [local(): lax.all_to_all(summed.reshape(owner_count, capacity, share_width), 'rep',...]
    psum x0 -> x1, blocking collectives: none -> 6.53 us  [local(): lax.psum(jnp.sum(hidden * hidden, axis=-1, keepdims=True), 'tp')]
  transfers between devices with their start and end apart: 3 -> 4, of which waited for: 3 -> 4; matrix products, arithmetic and copies ran while one was open for 1% -> 0% of each run, Pallas kernels for 0% -> 0%
where the time goes in v1:
time: 335 us; the launch traced here: 334 us
  waiting for transfers between devices  209 us (62%)
  blocking collectives  49 us (15%)
  matrix products  29.4 us (9%)
  local copies, waits for them, and re-layouts  20.3 us (6%)
  between operations  13.3 us (4%)
  other arithmetic  12.1 us (4%)
    reduce_scatter x1, waiting for transfers between devices, local(): moe = lax.psum_scatter(moe, 'rep', scatter_dimension=0, tiled=True)  80.5 us
    reduce_scatter x1, waiting for transfers between devices, local(): moe = lax.psum_scatter(expert_terms, 'tp', scatter_dimension=1, tiled=True)  79.8 us
    all_gather x1, blocking collectives, local(): spread_all = lax.all_gather(spread, 'rep', axis=0, tiled=True)  32.3 us
    all_gather x1, waiting for transfers between devices, local(): rows = lax.all_gather(rows, 'rep', axis=0, tiled=True)  26.8 us
    reduce_scatter x1, waiting for transfers between devices, local(): lax.psum_scatter(partial_out, 'tp', scatter_dimension=1, tiled=True)  22.4 us
    gather x1, local copies, waits for them, and re-layouts, local(): cache = jnp.take(kv_pool, page_table.reshape(-1), axis=2)  12 us
    all_gather x1, blocking collectives, local(): rows = lax.all_gather(normed, 'tp', axis=1, tiled=True)  10.1 us
    dot_general x1, matrix products, local(): gate = jnp.dot(rows, w_gate[0], preferred_element_type=jnp.float32)  7.97 us
  transfers between devices with their start and end apart: 4, of which 4 were waited for; matrix products, arithmetic and copies ran while one was open for 0% of the time, Pallas kernels for 0%

profile of v1, /device:TPU:1, one launch (start us, length us, event | category | flops | bytes accessed | tf_op | source)
XLA Modules:
  0.0 333.7 jit_solution(2013778808584484498)
XLA Ops:
  6.5 0.9 copy.23
  7.7 12.0 %gather_fusion = bf16[256,2,64,128]{3,2,1,0:T(8,128)(2,1)} fusion(bf16[2,256,64,128]{3,2,1,0:T(8,128)(2,1)} %bitcast.41, s32[1024]{0:T(1024)S(1)} %pad_clamp_fusion), kind=kCustom, calls=%fused_computation | custom fusion | bytes 16778240 | tf_op jit(solution)/shard_map/jit(_take)/gather | solution.py:41
  19.7 7.4 %bitcast_select_fusion = bf16[2,1,256,64,128]{4,3,0,2,1:T(8,128)(2,1)} fusion(bf16[256,2,64,128]{3,2,1,0:T(8,128)(2,1)} %gather_fusion, pred[256]{0:T(512)(128)(4,1)S(1)} %compare_and_fusion), kind=kLoop, calls=%fused_computation.3 | loop fusion | flops 4194304 | bytes 16777472 | tf_op jit(solution)/shard_map/jit(_take)/select_n | solution.py:41
  27.1 5.8 %fusion.16 = (bf16[1,1,256,64,128]{4,3,0,2,1:T(8,128)(2,1)S(1)}, bf16[1,1,256,64,128]{4,3,0,2,1:T(8,128)(2,1)}) fusion(bf16[2,1,256,64,128]{4,3,0,2,1:T(8,128)(2,1)} %bitcast_select_fusion), kind=kLoop, calls=%fused_computation.35 | loop fusion | bytes 16777216 | tf_op jit(solution)/shard_map/slice | solution.py:44
  33.1 1.2 fusion.11
  34.3 0.8 copy-done.1
  35.1 0.2 fusion.17
  35.3 3.2 convolution_convert_fusion
  38.6 5.8 %fusion.13 = f32[32,4096]{1,0:T(8,128)} fusion(bf16[1024,4096]{1,0:T(8,128)(2,1)} %param.17, bf16[4,8,8,128]{3,2,1,0:T(8,128)(2,1)S(1)} %bitcast.42), kind=kOutput, calls=%fused_computation.25 | convolution fusion | flops 268435456 | bytes 8978432 | tf_op jit(solution)/shard_map/dot_general | solution.py:53
  44.4 0.7 dynamic-slice_convert_fusion
  45.1 22.4 %reduce-scatter.4.cloned.1.call-done = f32[32,1024]{1,0:T(8,128)} async-done(((f32[32,4096]{1,0:T(8,128)}), f32[32,1024]{1,0:T(8,128)}) %reduce-scatter.4.cloned.1.call-update) | async-done | bytes 131088 | tf_op jit(solution)/shard_map/reduce_scatter | solution.py:54
  67.5 1.0 multiply_reduce_fusion
  68.5 6.5 %psum.7 = f32[32,1]{0,1:T(1,128)S(1)} all-reduce(f32[32,1]{0,1:T(1,128)S(1)} %bitcast.46), channel_id=1, replica_groups=mesh['rep'=32,'tp'=4] {'tp'}, use_global_device_ids=true, to_apply=%region_4.5 | all-reduce | flops 32 | bytes 256 | tf_op jit(solution)/shard_map/psum | solution.py:58
  75.1 1.0 multiply_convert_fusion.2
  76.1 10.1 %all_gather.9 = bf16[32,4096]{1,0:T(8,128)(2,1)} all-gather(bf16[32,1024]{1,0:T(8,128)(2,1)S(1)} %multiply_convert_fusion.2), channel_id=1, replica_groups=mesh['rep'=32,'tp'=4] {'tp'}, dimensions={1}, use_global_device_ids=true | all-gather | bytes 327680 | tf_op jit(solution)/shard_map/all_gather | solution.py:63
  86.6 32.3 %all_gather.11 = f32[1024,32]{1,0:T(8,128)S(1)} all-gather(f32[32,32]{1,0:T(8,128)S(1)} %select_reduce_fusion), channel_id=1, replica_groups=mesh['rep'=32,'tp'=4] {'rep'}, dimensions={0}, use_global_device_ids=true | all-gather | bytes 135168 | tf_op jit(solution)/shard_map/all_gather | solution.py:38
  118.9 0.4 dynamic-slice_reduce_fusion
  119.3 26.8 %all-gather.2.cloned.1.call-done = bf16[1024,4096]{1,0:T(8,128)(2,1)} async-done(((bf16[32,4096]{1,0:T(8,128)(2,1)}), bf16[1024,4096]{1,0:T(8,128)(2,1)}) %all-gather.2.cloned.1.call-update) | async-done | bytes 8388624 | tf_op jit(solution)/shard_map/all_gather | solution.py:64
  146.1 8.0 %fusion.4 = f32[1024,384]{1,0:T(8,128)S(1)} fusion(bf16[1024,4096]{1,0:T(8,128)(2,1)} %all-gather.2.cloned.1.call-done, bf16[1,4096,384]{2,1,0:T(8,128)(2,1)} %param.21), kind=kOutput, calls=%fused_computation.7 | convolution fusion | flops 3221225472 | bytes 13107200 | tf_op jit(solution)/shard_map/dot_general | solution.py:65
  154.1 4.6 %multiply_convert_fusion.1 = bf16[1024,384]{1,0:T(8,128)(2,1)S(1)} fusion(f32[1024,384]{1,0:T(8,128)S(1)} %fusion.4, bf16[1024,4096]{1,0:T(8,128)(2,1)S(1)} %copy-done.8, bf16[1,4096,384]{2,1,0:T(8,128)(2,1)S(1)} %copy-done.9), kind=kOutput, calls=%fused_computation.9 | convolution fusion | flops 3223584768 | bytes 13893632 | tf_op jit(solution)/shard_map/dot_general | solution.py:66
  158.7 6.7 %multiply_convert_fusion = bf16[1024,4096]{1,0:T(8,128)(2,1)} fusion(bf16[1024,384]{1,0:T(8,128)(2,1)S(1)} %multiply_convert_fusion.1, f32[1024]{0:T(1024)S(1)} %dynamic-slice_reduce_fusion, bf16[1,384,4096]{2,1,0:T(8,128)(2,1)S(1)} %copy-done), kind=kOutput, calls=%fused_computation.2 | convolution fusion | flops 3229614080 | bytes 12324864 | tf_op jit(solution)/shard_map/dot_general | solution.py:68
  165.4 79.8 %reduce-scatter.6.cloned.1.call-done = bf16[1024,1024]{1,0:T(8,128)(2,1)} async-done(((bf16[1024,4096]{1,0:T(8,128)(2,1)}), bf16[1024,1024]{1,0:T(8,128)(2,1)}) %reduce-scatter.6.cloned.1.call-update) | async-done | bytes 2097168 | tf_op jit(solution)/shard_map/reduce_scatter | solution.py:70
  245.2 80.5 %reduce-scatter.8.cloned.1.call-done = bf16[32,1024]{1,0:T(8,128)(2,1)} async-done(((bf16[1024,1024]{1,0:T(8,128)(2,1)}), bf16[32,1024]{1,0:T(8,128)(2,1)}) %reduce-scatter.8.cloned.1.call-update) | async-done | bytes 65552 | tf_op jit(solution)/shard_map/reduce_scatter | solution.py:71
  325.6 1.5 add_convert_fusion
  (38 shorter events, 0.8 us)
Async XLA Ops:
  6.5 152.1 %copy-start = (bf16[1,384,4096]{2,1,0:T(8,128)(2,1)S(1)}, bf16[1,384,4096]{2,1,0:T(8,128)(2,1)}, u32[]{:S(2)}) copy-start(bf16[1,384,4096]{2,1,0:T(8,128)(2,1)} %param.23) | copy-start | bytes 9437188
  6.5 61.0 %reduce-scatter.4.cloned.1.call-start = ((), (), s32[]{:S(2)}) async-start(), calls=%async_computation.3 | async-start | bytes 655360 | tf_op jit(solution)/shard_map/reduce_scatter | solution.py:54
  27.1 5.9 %copy-start.4 = (bf16[32,1024]{1,0:T(8,128)(2,1)S(1)}, bf16[32,1024]{1,0:T(8,128)(2,1)}, u32[]{:S(2)}) copy-start(bf16[32,1024]{1,0:T(8,128)(2,1)} %param.12) | copy-start | bytes 196612
  27.1 5.9 %copy-start.7 = (s32[32]{0:T(128)S(1)}, s32[32]{0:T(128)}, u32[]{:S(2)}) copy-start(s32[32]{0:T(128)} %param.15) | copy-start | bytes 388
  34.3 0.8 copy-start.1
  38.5 29.0 %copy-start.3 = (bf16[32,4096]{1,0:T(8,128)(2,1)S(1)}, bf16[32,4096]{1,0:T(8,128)(2,1)}, u32[]{:S(2)}) copy-start(bf16[32,4096]{1,0:T(8,128)(2,1)} %param.16) | copy-start | bytes 786436
  38.5 47.7 %copy-start.5 = (s32[32,8]{0,1:T(8,128)S(1)}, s32[32,8]{0,1:T(8,128)}, u32[]{:S(2)}) copy-start(s32[32,8]{0,1:T(8,128)} %param.19) | copy-start | bytes 3076
  38.6 47.8 %copy-start.6 = (f32[32,8]{0,1:T(8,128)S(1)}, f32[32,8]{0,1:T(8,128)}, u32[]{:S(2)}) copy-start(f32[32,8]{0,1:T(8,128)} %param.20) | copy-start | bytes 3076
  44.4 101.7 %all-gather.2.cloned.1.call-start = ((), (), s32[]{:S(2)}) async-start(), calls=%async_computation.4 | async-start | bytes 8650752 | tf_op jit(solution)/shard_map/all_gather | solution.py:64
  86.2 159.0 %reduce-scatter.6.cloned.1.call-start = ((), (), s32[]{:S(2)}) async-start(), calls=%async_computation.5 | async-start | bytes 10485760 | tf_op jit(solution)/shard_map/reduce_scatter | solution.py:70
  146.1 8.0 %copy-start.8 = (bf16[1024,4096]{1,0:T(8,128)(2,1)S(1)}, bf16[1024,4096]{1,0:T(8,128)(2,1)}, u32[]{:S(2)}) copy-start(bf16[1024,4096]{1,0:T(8,128)(2,1)} %all-gather.2.cloned.1.call-done) | copy-start | bytes 25165828
  146.1 8.0 %copy-start.9 = (bf16[1,4096,384]{2,1,0:T(8,128)(2,1)S(1)}, bf16[1,4096,384]{2,1,0:T(8,128)(2,1)}, u32[]{:S(2)}) copy-start(bf16[1,4096,384]{2,1,0:T(8,128)(2,1)} %param.22) | copy-start | bytes 9437188
  165.3 160.3 %copy-start.2 = (f32[32,1024]{1,0:T(8,128)S(1)}, f32[32,1024]{1,0:T(8,128)}, u32[]{:S(2)}) copy-start(f32[32,1024]{1,0:T(8,128)} %reduce-scatter.4.cloned.1.call-done) | copy-start | bytes 393220
  165.4 160.3 %reduce-scatter.8.cloned.1.call-start = ((), (), s32[]{:S(2)}) async-start(), calls=%async_computation.6 | async-start | bytes 2162688 | tf_op jit(solution)/shard_map/reduce_scatter | solution.py:71
Sparse Core Ops, SparseCore 0:
  44.5 22.9 reduce-scatter.3
  86.3 59.6 all-gather.1
  165.5 79.6 reduce-scatter.5
  248.6 77.0 reduce-scatter.7

commit v2 on v1

v2 whole, which is shorter than its diff:
```python
import functools

import jax
import jax.numpy as jnp
from jax import lax
from jax.experimental import pallas as pl
from jax.experimental.pallas import tpu as pltpu
from jax.sharding import PartitionSpec as P

norm_epsilon = 1e-06
MESH = pl.DeviceIdType.MESH
BF, F32 = jnp.bfloat16, jnp.float32
RING = 4
ROWS = 32
SHARE = 1024
HIDDEN = 384
ORDER = (("x", "y", "z"), ("y", "z", "x"), ("z", "x", "y"))
START = (0, 384, 768)
WIDE = (384, 384, 256)
CARRY = 384


def experts_kernel(
    part, residual, gain, ids, weights, w_gate, w_up, w_down, out,
    w_in, w_back, g0, g1, g2, acc, act, row_weight, hidden,
    p_in, sq_out, sq_in, y0, y1, y2, s0, s1, s2, l0, l1, l2, f0, f1, f2,
    t0, t1, t2, m0, m1, m2, u0, u1, u2, n0, n1, n2,
    send_sem, recv_sem, load_sem,
):
    rep, y = lax.axis_index("rep"), lax.axis_index("tp")
    x, z, core = rep // 8, (rep // 2) % 4, rep % 2
    at = {"x": x, "y": y, "z": z}
    G, Y, S = (g0, g1, g2), (y0, y1, y2), (s0, s1, s2)
    L, F, T, M, U, N = (l0, l1, l2), (f0, f1, f2), (t0, t1, t2), (m0, m1, m2), (u0, u1, u2), (n0, n1, n2)

    def near(axis, off):
        return lax.rem(at[axis] + off, RING)

    def peer(axis, off):
        c = dict(at)
        c[axis] = near(axis, off)
        return ((c["x"] * RING + c["z"]) * 2 + core, c["y"])

    twin = ((x * RING + z) * 2 + 1 - core, y)

    barrier = pltpu.get_barrier_semaphore()
    others = [peer(a, o) for a in "xyz" for o in (1, 2, 3)] + [twin]
    for other in others:
        pl.semaphore_signal(barrier, inc=1, device_id=other, device_id_type=MESH)

    loads = []
    for i, (src, dst) in enumerate((
        (w_gate.at[0], w_in.at[:, pl.ds(0, HIDDEN)]),
        (w_up.at[0], w_in.at[:, pl.ds(HIDDEN, HIDDEN)]),
        (w_down.at[0], w_back),
    )):
        load = pltpu.make_async_copy(src, dst, load_sem.at[i])
        load.start()
        loads.append(load)

    sends = []

    def send(src, dst, to):
        i = len(sends)
        copy = pltpu.make_async_remote_copy(
            src_ref=src, dst_ref=dst, send_sem=send_sem.at[i], recv_sem=recv_sem.at[i],
            device_id=to, device_id_type=MESH,
        )
        copy.start()
        sends.append(copy)
        return i

    def arrived(i, landing):
        pltpu.make_async_remote_copy(
            src_ref=landing, dst_ref=landing, send_sem=send_sem.at[i], recv_sem=recv_sem.at[i],
            device_id=twin, device_id_type=MESH,
        ).wait_recv()

    lane = lax.broadcasted_iota(jnp.int32, (ROWS, 128), 1)
    spread = jnp.zeros((ROWS, 128), F32)
    for k in range(8):
        spread = spread + jnp.where(lane % 32 == ids[:, k : k + 1], weights[:, k : k + 1], 0.0)
    top = spread.astype(BF).astype(F32)
    mid = (spread - top).astype(BF).astype(F32)
    low = spread - top - mid
    third = lane // 32
    spread = jnp.where(third == 0, top, jnp.where(third == 1, mid, jnp.where(third == 2, low, 0.0)))

    pl.semaphore_wait(barrier, len(others))

    ids_p = {}
    for o in (2, 1, 3):
        ids_p[o] = send(part.at[near("y", o)], p_in.at[o - 1], peer("y", o))
    acc[...] = jnp.zeros_like(acc)
    col = pl.ds(pl.multiple_of(y * SHARE, SHARE), SHARE)
    total = residual[:, col].astype(F32) + part[y].astype(F32)
    for o in (1, 3, 2):
        arrived(ids_p[o], p_in.at[o - 1])
        total = total + p_in[o - 1].astype(F32)
    hidden[...] = total
    square = jnp.sum(total * total, axis=1, keepdims=True)
    sq_out[...] = jnp.broadcast_to(square, (ROWS, 128))
    ids_q = {o: send(sq_out, sq_in.at[o - 1], peer("y", o)) for o in (2, 1, 3)}
    scaled_gain = gain[:, col].astype(F32)
    square = sq_out[...]
    for o in (1, 3, 2):
        arrived(ids_q[o], sq_in.at[o - 1])
        square = square + sq_in[o - 1]
    scale = lax.rsqrt(square[:, 0:1] * (1.0 / (RING * SHARE)) + norm_epsilon)
    normed = (hidden[...] * scale * scaled_gain).astype(BF)

    def block(p, i3, i2, first, count, c):
        inner = pl.ds(first, count)
        if p == 1:
            return G[p].at[i3, inner, i2, c]
        return G[p].at[i3, i2, inner, c]

    own = [tuple(at[a] for a in ORDER[p]) for p in range(3)]
    mine = (g0.at[z, y, x, core], g1.at[x, y, z, core], g2.at[y, x, z, core])
    for p in range(3):
        piece = normed[:, START[p] : START[p] + WIDE[p]]
        if WIDE[p] < CARRY:
            piece = jnp.concatenate([piece, spread.astype(BF)], axis=1)
        mine[p][...] = piece

    one = [{} for _ in range(3)]
    two = [{} for _ in range(3)]
    plain = [{} for _ in range(3)]
    relay = [{} for _ in range(3)]
    across = [{} for _ in range(3)]

    def to_twin(p, i3, i2, key):
        ref = block(p, i3, i2, 0, RING, core)
        across[p][key] = send(ref, ref, twin)

    def send_plain(p, s):
        q1, q2, q3 = own[p]
        ref = block(p, q3, near(ORDER[p][1], (4 - s) % 4), 0, RING, core)
        for o in (1, 3):
            plain[p][s, o] = send(ref, ref, peer(ORDER[p][2], o))
        to_twin(p, q3, near(ORDER[p][1], (4 - s) % 4), (0, s))

    for p in range(3):
        q1, q2, q3 = own[p]
        ref = block(p, q3, q2, q1, 1, core)
        for o in (1, 3, 2):
            one[p][o] = send(ref, ref, peer(ORDER[p][0], o))
    for p in range(3):
        q1, q2, q3 = own[p]
        for o in (1, 3, 2):
            arrived(one[p][o], block(p, q3, q2, near(ORDER[p][0], 4 - o), 1, core))
        ref = block(p, q3, q2, 0, RING, core)
        for o in (1, 3, 2):
            two[p][o] = send(ref, ref, peer(ORDER[p][1], o))
        send_plain(p, 0)
    for o in (1, 3, 2):
        for p in range(3):
            q1, q2, q3 = own[p]
            arrived(two[p][o], block(p, q3, near(ORDER[p][1], 4 - o), 0, RING, core))
            send_plain(p, o)

    def pass_on(s):
        for p in range(3):
            i2 = near(ORDER[p][1], (4 - s) % 4)
            for o in (1, 3):
                i3 = near(ORDER[p][2], 4 - o)
                arrived(plain[p][s, o], block(p, i3, i2, 0, RING, core))
                ref = block(p, i3, i2, 0 if o == 1 else 2, 2, core)
                relay[p][s, o] = send(ref, ref, peer(ORDER[p][2], o))
                to_twin(p, i3, i2, (o, s))

    def last_in(s):
        for p in range(3):
            i2 = near(ORDER[p][1], (4 - s) % 4)
            i3 = near(ORDER[p][2], 2)
            arrived(relay[p][s, 1], block(p, i3, i2, 0, 2, core))
            arrived(relay[p][s, 3], block(p, i3, i2, 2, 2, core))
            to_twin(p, i3, i2, (2, s))

    def twin_in(p, d):
        i3 = near(ORDER[p][2], (4 - d) % 4)
        for s in (0, 1, 3, 2):
            i2 = near(ORDER[p][1], (4 - s) % 4)
            arrived(across[p][d, s], block(p, i3, i2, 0, RING, 1 - core))
        return i3

    def project(p, d):
        i3 = twin_in(p, d)
        width = WIDE[p]

        def columns(n, _):
            c = pl.ds(pl.multiple_of(n * 256, 256), 256)
            if p == 2:
                w = w_in[pl.ds(pl.multiple_of(i3 * SHARE + START[2], 256), width), c]
                for i in range(RING):
                    rows = g2[i3, i, :, :, :, 0:width].reshape(256, width)
                    acc[i, :, :, c] += jnp.dot(rows, w, preferred_element_type=F32).reshape(RING, 64, 256)
                return 0
            total = jnp.zeros((256, 256), F32)
            for t in range(RING):
                rows = G[p][i3, t].reshape(256, width)
                w = w_in[t * SHARE + START[p] : t * SHARE + START[p] + width, c]
                total = total + jnp.dot(rows, w, preferred_element_type=F32)
            total = total.reshape(RING, 64, 256)
            if p == 0:
                acc[:, i3, :, c] += total
            else:
                acc[i3, :, :, c] += total
            return 0

        lax.fori_loop(0, 3, columns, 0)

    pass_on(0)
    loads[0].wait()
    loads[1].wait()
    project(0, 0)
    pass_on(1)
    project(1, 0)
    pass_on(3)
    project(2, 0)
    pass_on(2)
    last_in(0)
    project(0, 1)
    project(1, 1)
    last_in(1)
    project(2, 1)
    project(0, 3)
    last_in(3)
    project(1, 3)
    project(2, 3)
    last_in(2)
    for p in range(3):
        project(p, 2)

    pick = lax.broadcasted_iota(jnp.int32, (128, 128), 0)
    pick = jnp.where((pick % 32 == rep) & (pick < 96), 1.0, 0.0).astype(BF)

    def units(i, _):
        table = g2[y, i, :, :, :, 256:384].reshape(256, 128)
        row_weight[i] = jnp.dot(table, pick, preferred_element_type=F32).reshape(RING, 64, 128)
        g = acc[i, :, :, 0:HIDDEN]
        u = acc[i, :, :, HIDDEN : 2 * HIDDEN]
        act[i] = (g / (1.0 + jnp.exp(-g)) * u).astype(BF)
        return 0

    lax.fori_loop(0, RING, units, 0)
    loads[2].wait()

    def sub(p, ref, i2, first, count):
        inner = pl.ds(first, count)
        if p == 1:
            return ref.at[inner, i2]
        return ref.at[i2, inner]

    def weighted(value, w, width):
        return jnp.concatenate(
            [value[:, j * 128 : (j + 1) * 128] * w for j in range(width // 128)], axis=1
        ).astype(BF)

    crossed = [{} for _ in range(3)]

    def back(p, d):
        i3 = near(ORDER[p][2], d)
        width = WIDE[p]
        if p == 2:
            w = w_back[:, pl.ds(pl.multiple_of(i3 * SHARE + START[2], 256), width)]

            def body(i, _):
                value = jnp.dot(act[i].reshape(256, HIDDEN), w, preferred_element_type=F32)
                value = weighted(value, row_weight[i].reshape(256, 128), width).reshape(RING, 2, ROWS, width)
                for k in range(2):
                    y2[k, i3, i] = value[:, k]
                return 0

            lax.fori_loop(0, RING, body, 0)
        else:
            if p == 0:
                a = act[:, i3].reshape(256, HIDDEN)
                rw = row_weight[:, i3].reshape(256, 128)
            else:
                a = act[i3].reshape(256, HIDDEN)
                rw = row_weight[i3].reshape(256, 128)

            def body(t, _):
                w = w_back[:, pl.ds(pl.multiple_of(t * SHARE + START[p], 128), width)]
                value = jnp.dot(a, w, preferred_element_type=F32)
                value = weighted(value, rw, width).reshape(RING, 2, ROWS, width)
                for k in range(2):
                    Y[p][k, i3, t] = value[:, k]
                return 0

            lax.fori_loop(0, RING, body, 0)
        crossed[p][d] = send(Y[p].at[1 - core, i3], S[p].at[i3], twin)

    def add_twin(p, d):
        i3 = near(ORDER[p][2], d)
        arrived(crossed[p][d], S[p].at[i3])

        def body(i, _):
            Y[p][core, i3, i] = (Y[p][core, i3, i].astype(F32) + S[p][i3, i].astype(F32)).astype(BF)
            return 0

        lax.fori_loop(0, RING, body, 0)

    handed = [{} for _ in range(3)]
    direct = [{} for _ in range(3)]

    def hand_out(p):
        i3 = near(ORDER[p][2], 2)
        for s in (2, 1, 3, 0):
            i2 = near(ORDER[p][1], s)
            for k, o in enumerate((1, 3)):
                handed[p][s, o] = send(sub(p, Y[p].at[core, i3], i2, 2 * k, 2), L[p].at[k, s], peer(ORDER[p][2], o))

    def forward(p, s):
        i2 = near(ORDER[p][1], s)
        for k, o in enumerate((1, 3)):
            i3 = near(ORDER[p][2], o)
            arrived(handed[p][s, o], L[p].at[k, s])
            ref = sub(p, Y[p].at[core, i3], i2, 2 * k, 2)
            ref[...] = (ref[...].astype(F32) + L[p][k, s].astype(F32)).astype(BF)
            direct[p][s, o] = send(sub(p, Y[p].at[core, i3], i2, 0, RING), F[p].at[k, s], peer(ORDER[p][2], o))

    second = [{} for _ in range(3)]
    third_ids = [{} for _ in range(3)]

    def collect(p, s):
        i2 = near(ORDER[p][1], s)
        for k, o in enumerate((1, 3)):
            arrived(direct[p][s, o], F[p].at[k, s])
        value = sub(p, Y[p].at[core, own[p][2]], i2, 0, RING)[...].astype(F32)
        T[p][s] = (value + F[p][0, s].astype(F32) + F[p][1, s].astype(F32)).astype(BF)
        if s:
            second[p][s] = send(T[p].at[s], M[p].at[s - 1], peer(ORDER[p][1], s))

    def collect_line(p):
        value = T[p][0].astype(F32)
        for s in (1, 3, 2):
            arrived(second[p][s], M[p].at[s - 1])
            value = value + M[p][s - 1].astype(F32)
        U[p][...] = value.astype(BF)
        for o in (2, 1, 3):
            third_ids[p][o] = send(U[p].at[near(ORDER[p][0], o)], N[p].at[o - 1], peer(ORDER[p][0], o))

    for p in range(3):
        back(p, 2)
    for p in range(3):
        add_twin(p, 2)
        hand_out(p)
    for d in (1, 3, 0):
        for p in range(3):
            back(p, d)
    for p in range(3):
        add_twin(p, 1)
        add_twin(p, 3)
    for s in (2, 1, 3, 0):
        for p in range(3):
            forward(p, s)
    for p in range(3):
        add_twin(p, 0)
    for s in (2, 1, 3, 0):
        for p in range(3):
            collect(p, s)
    for p in range(3):
        collect_line(p)
    for p in range(3):
        value = U[p][own[p][0]].astype(F32)
        for o in (1, 3, 2):
            arrived(third_ids[p][o], N[p].at[o - 1])
            value = value + N[p][o - 1].astype(F32)
        c = slice(START[p], START[p] + WIDE[p])
        out[:, c] = (hidden[:, c] + value).astype(BF)

    for copy in sends:
        copy.wait_send()


SEMS = 6 + 3 * (3 + 3 + 8 + 8 + 16) + 3 * (4 + 8 + 8 + 3 + 3)


def experts(part, residual, gain, ids, weights, w_gate, w_up, w_down):
    vmem = pl.BlockSpec(memory_space=pltpu.VMEM)
    hbm = pl.BlockSpec(memory_space=pl.ANY)
    V = pltpu.VMEM
    R = RING
    scratch = [
        V((R * SHARE, 2 * HIDDEN), BF),
        V((HIDDEN, R * SHARE), BF),
        V((R, R, R, 2, ROWS, CARRY), BF),
        V((R, R, R, 2, ROWS, CARRY), BF),
        V((R, R, R, 2, ROWS, CARRY), BF),
        V((R, R, 2 * ROWS, 2 * HIDDEN), F32),
        V((R, R, 2 * ROWS, HIDDEN), BF),
        V((R, R, 2 * ROWS, 128), F32),
        V((ROWS, SHARE), F32),
        V((3, ROWS, SHARE), BF),
        V((ROWS, 128), F32),
        V((3, ROWS, 128), F32),
    ]
    scratch += [V((2, R, R, R, ROWS, w), BF) for w in WIDE]
    scratch += [V((R, R, R, ROWS, w), BF) for w in WIDE]
    scratch += [V((2, R, 2, ROWS, w), BF) for w in WIDE]
    scratch += [V((2, R, R, ROWS, w), BF) for w in WIDE]
    scratch += [V((R, R, ROWS, w), BF) for w in WIDE]
    scratch += [V((3, R, ROWS, w), BF) for w in WIDE]
    scratch += [V((R, ROWS, w), BF) for w in WIDE]
    scratch += [V((3, ROWS, w), BF) for w in WIDE]
    scratch += [pltpu.SemaphoreType.DMA((SEMS,)), pltpu.SemaphoreType.DMA((SEMS,)), pltpu.SemaphoreType.DMA((3,))]
    return pl.pallas_call(
        experts_kernel,
        out_shape=jax.ShapeDtypeStruct((ROWS, SHARE), BF),
        in_specs=[vmem] * 5 + [hbm] * 3,
        out_specs=vmem,
        scratch_shapes=scratch,
        compiler_params=pltpu.CompilerParams(
            collective_id=0, has_side_effects=True, vmem_limit_bytes=56 * 1024 * 1024
        ),
    )(part, residual, gain, ids, weights, w_gate, w_up, w_down)


def local(
    query, kv_pool, page_table, lengths, residual, w_out, norm_gain,
    route_ids, route_weights, w_gate, w_up, w_down,
):
    row_count = query.shape[0]
    kv_local = kv_pool.shape[1]
    page_len = kv_pool.shape[3]
    head_dim = kv_pool.shape[4]
    group_size = query.shape[1] // (kv_local * head_dim)
    context = page_table.shape[1] * page_len
    cache = jnp.take(kv_pool, page_table.reshape(-1), axis=2)
    cache = cache.reshape(2, kv_local, row_count, context, head_dim)
    queries = query.reshape(row_count, kv_local, group_size, head_dim)
    scores = jnp.einsum("rkgd,krcd->rkgc", queries, cache[0], preferred_element_type=jnp.float32)
    scores = scores * head_dim ** (-0.5)
    valid_keys = jnp.arange(context, dtype=jnp.int32)[None, :] < lengths[:, None]
    scores = jnp.where(valid_keys[:, None, None, :], scores, -1e30)
    top_score = jnp.max(scores, axis=-1, keepdims=True)
    weights = jnp.exp(scores - top_score)
    probs = (weights / jnp.sum(weights, axis=-1, keepdims=True)).astype(jnp.bfloat16)
    mixed = jnp.einsum("rkgc,krcd->rkgd", probs, cache[1], preferred_element_type=jnp.float32)
    attn = mixed.reshape(row_count, kv_local * group_size * head_dim).astype(jnp.bfloat16)
    part = jnp.einsum("rf,fts->trs", attn, w_out.reshape(-1, RING, SHARE), preferred_element_type=jnp.float32)
    return experts(
        part.astype(BF), residual, norm_gain.reshape(1, -1), route_ids, route_weights, w_gate, w_up, w_down
    )


def solution(mesh):
    in_specs = (
        P("rep", "tp"),
        P(None, "tp", "rep", None, None),
        P("rep", None),
        P("rep"),
        P("rep", None),
        P("tp", None),
        P(),
        P("rep", None),
        P("rep", None),
        P("rep", None, "tp"),
        P("rep", None, "tp"),
        P("rep", "tp", None),
    )
    out_specs = P("rep", "tp")
    return jax.shard_map(local, mesh=mesh, in_specs=in_specs, out_specs=out_specs, check_vma=False)
```

time: 335 us -> 127 us (0.38)
  waiting for transfers between devices: 209 us -> 0 us
  Pallas kernels: 0 us -> 86.2 us
  blocking collectives: 49 us -> 0 us
  matrix products: 29.4 us -> 9.72 us
  between operations: 13.3 us -> 0.07 us
  other arithmetic: 12.1 us -> 7.78 us
    reduce_scatter x3 -> x0, waiting for transfers between devices: 183 us -> none  [the longest x1 80.5 us: local(): moe = lax.psum_scatter(moe, 'rep', scatter_dimension=0, tiled=True)]
    pallas_call x0 -> x1, Pallas kernels: none -> 86.2 us  [experts(): pl.pallas_call(experts_kernel, out_shape=jax.ShapeDtypeStruct((ROWS, SHAR...]
    all_gather x2 -> x0, blocking collectives: 42.4 us -> none  [the longest x1 32.3 us: local(): spread_all = lax.all_gather(spread, 'rep', axis=0, tiled=True)]
    all_gather x1 -> x0, waiting for transfers between devices: 26.8 us -> none  [local(): rows = lax.all_gather(rows, 'rep', axis=0, tiled=True)]
    dot_general x4 -> x1, matrix products: 25 us -> 5.63 us  [local(): jnp.einsum('rf,fts->trs', attn, w_out.reshape(-1, RING, SHARE), preferred...]
    psum x1 -> x0, blocking collectives: 6.53 us -> none  [local(): lax.psum(jnp.sum(hidden * hidden, axis=-1, keepdims=True), 'tp')]
  transfers between devices with their start and end apart: 4 -> 0, of which waited for: 4 -> 0; matrix products, arithmetic and copies ran while one was open for 0% -> 0% of each run, Pallas kernels for 0% -> 0%
where the time goes in v2:
time: 127 us; the launch traced here: 126 us
  Pallas kernels  86.2 us (68%)
  local copies, waits for them, and re-layouts  22.3 us (18%)
  matrix products  9.72 us (8%)
  other arithmetic  7.78 us (6%)
    pallas_call x1, Pallas kernels, experts(): pl.pallas_call(experts_kernel, out_shape=jax.ShapeDtypeStruct((ROWS, SHAR...  86.2 us
    gather x1, local copies, waits for them, and re-layouts, local(): cache = jnp.take(kv_pool, page_table.reshape(-1), axis=2)  12 us
    select_n x2, other arithmetic, local(): cache = jnp.take(kv_pool, page_table.reshape(-1), axis=2)  7.45 us
    slice x1, local copies, waits for them, and re-layouts, local(): cache[0]  5.85 us
    dot_general x1, matrix products, local(): jnp.einsum('rf,fts->trs', attn, w_out.reshape(-1, RING, SHARE), preferred...  5.63 us
    unnamed x15, local copies, waits for them, and re-layouts  3.62 us
    dot_general x1, matrix products, local(): jnp.einsum('rkgc,krcd->rkgd', probs, cache[1], preferred_element_type=jnp...  2.9 us

profile of v2, /device:TPU:1, one launch (start us, length us, event | category | flops | bytes accessed | tf_op | source)
XLA Modules:
  0.0 126.1 jit_solution(14662628252214047271)
XLA Ops:
  0.0 0.8 copy.16
  0.8 0.1 reshape.114
  0.9 12.0 %gather_fusion = bf16[256,2,64,128]{3,2,1,0:T(8,128)(2,1)} fusion(bf16[2,256,64,128]{3,2,1,0:T(8,128)(2,1)} %bitcast.30, s32[1024]{0:T(1024)S(1)} %pad_clamp_fusion), kind=kCustom, calls=%fused_computation | custom fusion | bytes 16778240 | tf_op jit(solution)/shard_map/jit(_take)/gather | solution.py:431
  12.9 0.1 reshape.113
  13.0 7.4 %bitcast_select_fusion = bf16[2,1,256,64,128]{4,3,0,2,1:T(8,128)(2,1)} fusion(bf16[256,2,64,128]{3,2,1,0:T(8,128)(2,1)} %gather_fusion, pred[256]{0:T(512)(128)(4,1)S(1)} %compare_and_fusion), kind=kLoop, calls=%fused_computation.5 | loop fusion | flops 4194304 | bytes 16777472 | tf_op jit(solution)/shard_map/jit(_take)/select_n | solution.py:431
  20.4 0.0 copy-start
  20.4 0.0 copy-start.4
  20.4 5.8 %fusion.15 = (bf16[1,1,256,64,128]{4,3,0,2,1:T(8,128)(2,1)S(1)}, bf16[1,1,256,64,128]{4,3,0,2,1:T(8,128)(2,1)}) fusion(bf16[2,1,256,64,128]{4,3,0,2,1:T(8,128)(2,1)} %bitcast_select_fusion), kind=kLoop, calls=%fused_computation.21 | loop fusion | bytes 16777216 | tf_op jit(solution)/shard_map/slice | solution.py:434
  26.3 0.0 copy-done
  26.3 0.0 copy-done.4
  26.3 0.1 iota_compare_fusion
  26.4 1.2 fusion.7
  27.6 0.0 copy-start.1
  27.6 0.2 fusion.16
  27.8 2.9 %convolution_convert_fusion = bf16[32,8,128]{2,1,0:T(8,128)(2,1)S(1)} fusion(bf16[32,512,128]{2,1,0:T(8,128)(2,1)} %bitcast.28, f32[32,8]{1,0:T(8,128)S(1)} %fusion.16, f32[32,8,512]{2,1,0:T(8,128)S(1)} %fusion.7), kind=kOutput, calls=%fused_computation.13 | convolution fusion | flops 33981184 | bytes 4785152 | tf_op jit(solution)/shard_map/rkgc,krcd->rkgd/dot_general | solution.py:441
  30.8 5.6 %fusion.11.part = bf16[4,32,1024]{2,1,0:T(8,128)(2,1)} fusion(bf16[32,1024,1]{1,0,2:T(8,128)(2,1)S(1)} %reshape.130, bf16[128,4,8,1024]{3,2,1,0:T(8,128)(2,1)} %bitcast.34), kind=kOutput, calls=%fused_computation.12 | convolution fusion | flops 268566528 | bytes 8716288 | tf_op jit(solution)/shard_map/rf,fts->trs/dot_general | solution.py:443
  36.4 0.0 copy-done.2
  36.4 0.7 copy.19.ids
  37.1 0.0 copy-done.3
  37.1 0.7 copy.20.weights
  37.8 0.0 copy-done.1
  37.8 0.6 reshape.119.gain
  38.4 86.2 %shard_map.118 = bf16[32,1024]{1,0:T(8,128)(2,1)} custom-call(bf16[4,32,1024]{2,1,0:T(8,128)(2,1)} %fusion.11.part, bf16[32,4096]{1,0:T(8,128)(2,1)} %residual.1, bf16[1,4096]{1,0:T(2,128)(2,1)} %reshape.119.gain, s32[32,8]{1,0:T(8,128)} %copy.19.ids, f32[32,8]{1,0:T(8,128)} %copy.20.weights, bf16[1,4096,384]{2,1,0:T(8,128)(2,1)} %w_gate.1, ...), custom_call_target="tpu_custom_call" | custom-call | tf_op jit(solution)/shard_map/pallas_call | solution.py:409
  124.6 1.5 %copy.32 = bf16[32,1024]{1,0:T(8,128)(2,1)} copy(bf16[32,1024]{1,0:T(8,128)(2,1)} %shard_map.118) | data formatting | bytes 131072
  (7 shorter events, 0.1 us)
Async XLA Ops:
  20.4 5.9 %copy-start = (bf16[32,1024]{1,0:T(8,128)(2,1)S(1)}, bf16[32,1024]{1,0:T(8,128)(2,1)}, u32[]{:S(2)}) copy-start(bf16[32,1024]{1,0:T(8,128)(2,1)} %param.12) | copy-start | bytes 196612
  20.4 5.9 %copy-start.4 = (s32[32]{0:T(128)S(1)}, s32[32]{0:T(128)}, u32[]{:S(2)}) copy-start(s32[32]{0:T(128)} %param.15) | copy-start | bytes 388
  27.6 8.8 %copy-start.2 = (s32[32,8]{0,1:T(8,128)S(1)}, s32[32,8]{0,1:T(8,128)}, u32[]{:S(2)}) copy-start(s32[32,8]{0,1:T(8,128)} %param.19) | copy-start | bytes 3076
  27.6 9.5 %copy-start.3 = (f32[32,8]{0,1:T(8,128)S(1)}, f32[32,8]{0,1:T(8,128)}, u32[]{:S(2)}) copy-start(f32[32,8]{0,1:T(8,128)} %param.20) | copy-start | bytes 3076
  27.6 10.2 %copy-start.1 = (bf16[4096]{0:T(1024)(128)(2,1)S(1)}, bf16[4096]{0:T(1024)(128)(2,1)}, u32[]{:S(2)}) copy-start(bf16[4096]{0:T(1024)(128)(2,1)} %param.18) | copy-start | bytes 24580

commit v3 on v2

--- a/solution.py
+++ b/solution.py
@@ -13,6 +13,11 @@
 RING = 4
 ROWS = 32
 SHARE = 1024
+GROUP = 8
+HEAD = 128
+PAGE = 64
+PAGES = 256
+CONTEXT = 512
 HIDDEN = 384
 ORDER = (("x", "y", "z"), ("y", "z", "x"), ("z", "x", "y"))
 START = (0, 384, 768)
@@ -20,8 +25,9 @@
 CARRY = 384
 
 
-def experts_kernel(
-    part, residual, gain, ids, weights, w_gate, w_up, w_down, out,
+def layer_kernel(
+    query, kv, pages, lengths, residual, w_out, gain, ids, weights, w_gate, w_up, w_down, out,
+    k_in, v_in, w_proj, queries, scores, mixed, part, gains,
     w_in, w_back, g0, g1, g2, acc, act, row_weight, hidden,
     p_in, sq_out, sq_in, y0, y1, y2, s0, s1, s2, l0, l1, l2, f0, f1, f2,
     t0, t1, t2, m0, m1, m2, u0, u1, u2, n0, n1, n2,
@@ -41,6 +47,8 @@
         c[axis] = near(axis, off)
         return ((c["x"] * RING + c["z"]) * 2 + core, c["y"])
 
+    own = [tuple(at[a] for a in ORDER[p]) for p in range(3)]
+    mine = (g0.at[z, y, x, core], g1.at[x, y, z, core], g2.at[y, x, z, core])
     twin = ((x * RING + z) * 2 + 1 - core, y)
 
     barrier = pltpu.get_barrier_semaphore()
@@ -50,6 +58,9 @@
 
     loads = []
     for i, (src, dst) in enumerate((
+        (kv.at[0, 0], k_in),
+        (kv.at[1, 0], v_in),
+        (w_out, w_proj),
         (w_gate.at[0], w_in.at[:, pl.ds(0, HIDDEN)]),
         (w_up.at[0], w_in.at[:, pl.ds(HIDDEN, HIDDEN)]),
         (w_down.at[0], w_back),
@@ -76,24 +87,64 @@
             device_id=twin, device_id_type=MESH,
         ).wait_recv()
 
-    lane = lax.broadcasted_iota(jnp.int32, (ROWS, 128), 1)
-    spread = jnp.zeros((ROWS, 128), F32)
+    for h in range(GROUP):
+        queries[h * ROWS : (h + 1) * ROWS, :] = query[:, h * HEAD : (h + 1) * HEAD].astype(F32)
+    position = lax.broadcasted_iota(jnp.int32, (GROUP, CONTEXT), 1)
+
+    place = lax.broadcasted_iota(jnp.int32, (128, ROWS), 0)
+    spread = jnp.zeros((128, ROWS), F32)
     for k in range(8):
-        spread = spread + jnp.where(lane % 32 == ids[:, k : k + 1], weights[:, k : k + 1], 0.0)
+        spread = spread + jnp.where(place % 32 == ids[k : k + 1, :], weights[k : k + 1, :], 0.0)
     top = spread.astype(BF).astype(F32)
     mid = (spread - top).astype(BF).astype(F32)
     low = spread - top - mid
-    third = lane // 32
+    third = place // 32
     spread = jnp.where(third == 0, top, jnp.where(third == 1, mid, jnp.where(third == 2, low, 0.0)))
-
-    pl.semaphore_wait(barrier, len(others))
+    unit = jnp.where(
+        lax.broadcasted_iota(jnp.int32, (ROWS, ROWS), 0) == lax.broadcasted_iota(jnp.int32, (ROWS, ROWS), 1), 1.0, 0.0
+    ).astype(BF)
+    spread = lax.dot_general(unit, spread.astype(BF), (((1,), (1,)), ((), ())), preferred_element_type=F32)
+    mine[2][:, WIDE[2] :] = spread.astype(BF)
+    gains[...] = gain[...].astype(F32)
+
+    def row_pages(store, b):
+        return jnp.concatenate([store[pages[j, b]] for j in range(CONTEXT // PAGE)], axis=0)
+
+    def score(b, _):
+        q = queries[pl.ds(b, GROUP, stride=ROWS), :].astype(BF)
+        s = lax.dot_general(q, row_pages(k_in, b), (((1,), (1,)), ((), ())), preferred_element_type=F32)
+        s = jnp.where(position < lengths[b], s * HEAD ** -0.5, -1e30)
+        scores[pl.ds(pl.multiple_of(b * GROUP, GROUP), GROUP), :] = s
+        return 0
+
+    def mix(b, _):
+        p = scores[pl.ds(pl.multiple_of(b * GROUP, GROUP), GROUP), :].astype(BF)
+        mixed[pl.ds(b, GROUP, stride=ROWS), :] = jnp.dot(p, row_pages(v_in, b), preferred_element_type=F32)
+        return 0
+
+    loads[0].wait()
+    lax.fori_loop(0, ROWS, score, 0, unroll=4)
+    s = scores[...]
+    s = jnp.exp(s - jnp.max(s, axis=1, keepdims=True))
+    scores[...] = s / jnp.sum(s, axis=1, keepdims=True)
+    loads[1].wait()
+    lax.fori_loop(0, ROWS, mix, 0, unroll=4)
+    attn = jnp.concatenate([mixed[h * ROWS : (h + 1) * ROWS, :].astype(BF) for h in range(GROUP)], axis=1)
+    loads[2].wait()
+
+    def term(t):
+        w = w_proj[:, pl.ds(pl.multiple_of(t * SHARE, SHARE), SHARE)]
+        return jnp.dot(attn, w, preferred_element_type=F32)
 
     ids_p = {}
     for o in (2, 1, 3):
-        ids_p[o] = send(part.at[near("y", o)], p_in.at[o - 1], peer("y", o))
+        part[o - 1] = term(near("y", o)).astype(BF)
+        if o == 2:
+            pl.semaphore_wait(barrier, len(others))
+        ids_p[o] = send(part.at[o - 1], p_in.at[o - 1], peer("y", o))
     acc[...] = jnp.zeros_like(acc)
     col = pl.ds(pl.multiple_of(y * SHARE, SHARE), SHARE)
-    total = residual[:, col].astype(F32) + part[y].astype(F32)
+    total = residual[:, col].astype(F32) + term(y)
     for o in (1, 3, 2):
         arrived(ids_p[o], p_in.at[o - 1])
         total = total + p_in[o - 1].astype(F32)
@@ -101,13 +152,15 @@
     square = jnp.sum(total * total, axis=1, keepdims=True)
     sq_out[...] = jnp.broadcast_to(square, (ROWS, 128))
     ids_q = {o: send(sq_out, sq_in.at[o - 1], peer("y", o)) for o in (2, 1, 3)}
-    scaled_gain = gain[:, col].astype(F32)
     square = sq_out[...]
     for o in (1, 3, 2):
         arrived(ids_q[o], sq_in.at[o - 1])
         square = square + sq_in[o - 1]
     scale = lax.rsqrt(square[:, 0:1] * (1.0 / (RING * SHARE)) + norm_epsilon)
-    normed = (hidden[...] * scale * scaled_gain).astype(BF)
+    own_gain = jnp.concatenate(
+        [gains[pl.ds(y * (SHARE // 128) + j, 1), :] for j in range(SHARE // 128)], axis=1
+    )
+    normed = (hidden[...] * scale * own_gain).astype(BF)
 
     def block(p, i3, i2, first, count, c):
         inner = pl.ds(first, count)
@@ -115,13 +168,8 @@
             return G[p].at[i3, inner, i2, c]
         return G[p].at[i3, i2, inner, c]
 
-    own = [tuple(at[a] for a in ORDER[p]) for p in range(3)]
-    mine = (g0.at[z, y, x, core], g1.at[x, y, z, core], g2.at[y, x, z, core])
-    for p in range(3):
-        piece = normed[:, START[p] : START[p] + WIDE[p]]
-        if WIDE[p] < CARRY:
-            piece = jnp.concatenate([piece, spread.astype(BF)], axis=1)
-        mine[p][...] = piece
+    for p in range(3):
+        mine[p][:, 0 : WIDE[p]] = normed[:, START[p] : START[p] + WIDE[p]]
 
     one = [{} for _ in range(3)]
     two = [{} for _ in range(3)]
@@ -211,8 +259,8 @@
         lax.fori_loop(0, 3, columns, 0)
 
     pass_on(0)
-    loads[0].wait()
-    loads[1].wait()
+    loads[3].wait()
+    loads[4].wait()
     project(0, 0)
     pass_on(1)
     project(1, 0)
@@ -244,7 +292,7 @@
         return 0
 
     lax.fori_loop(0, RING, units, 0)
-    loads[2].wait()
+    loads[5].wait()
 
     def sub(p, ref, i2, first, count):
         inner = pl.ds(first, count)
@@ -378,12 +426,21 @@
 SEMS = 6 + 3 * (3 + 3 + 8 + 8 + 16) + 3 * (4 + 8 + 8 + 3 + 3)
 
 
-def experts(part, residual, gain, ids, weights, w_gate, w_up, w_down):
+def layer(*operands):
+    smem = pl.BlockSpec(memory_space=pltpu.SMEM)
     vmem = pl.BlockSpec(memory_space=pltpu.VMEM)
     hbm = pl.BlockSpec(memory_space=pl.ANY)
     V = pltpu.VMEM
     R = RING
     scratch = [
+        V((PAGES, PAGE, HEAD), BF),
+        V((PAGES, PAGE, HEAD), BF),
+        V((SHARE, R * SHARE), BF),
+        V((GROUP * ROWS, HEAD), F32),
+        V((GROUP * ROWS, CONTEXT), F32),
+        V((GROUP * ROWS, HEAD), F32),
+        V((3, ROWS, SHARE), BF),
+        V((32, 128), F32),
         V((R * SHARE, 2 * HIDDEN), BF),
         V((HIDDEN, R * SHARE), BF),
         V((R, R, R, 2, ROWS, CARRY), BF),
@@ -405,44 +462,26 @@
     scratch += [V((3, R, ROWS, w), BF) for w in WIDE]
     scratch += [V((R, ROWS, w), BF) for w in WIDE]
     scratch += [V((3, ROWS, w), BF) for w in WIDE]
-    scratch += [pltpu.SemaphoreType.DMA((SEMS,)), pltpu.SemaphoreType.DMA((SEMS,)), pltpu.SemaphoreType.DMA((3,))]
+    scratch += [pltpu.SemaphoreType.DMA((SEMS,)), pltpu.SemaphoreType.DMA((SEMS,)), pltpu.SemaphoreType.DMA((6,))]
     return pl.pallas_call(
-        experts_kernel,
+        layer_kernel,
         out_shape=jax.ShapeDtypeStruct((ROWS, SHARE), BF),
-        in_specs=[vmem] * 5 + [hbm] * 3,
+        in_specs=[vmem, hbm, smem, smem, vmem, hbm] + [vmem] * 3 + [hbm] * 3,
         out_specs=vmem,
         scratch_shapes=scratch,
         compiler_params=pltpu.CompilerParams(
-            collective_id=0, has_side_effects=True, vmem_limit_bytes=56 * 1024 * 1024
+            collective_id=0, has_side_effects=True, vmem_limit_bytes=61 * 1024 * 1024
         ),
-    )(part, residual, gain, ids, weights, w_gate, w_up, w_down)
+    )(*operands)
 
 
 def local(
     query, kv_pool, page_table, lengths, residual, w_out, norm_gain,
     route_ids, route_weights, w_gate, w_up, w_down,
 ):
-    row_count = query.shape[0]
-    kv_local = kv_pool.shape[1]
-    page_len = kv_pool.shape[3]
-    head_dim = kv_pool.shape[4]
-    group_size = query.shape[1] // (kv_local * head_dim)
-    context = page_table.shape[1] * page_len
-    cache = jnp.take(kv_pool, page_table.reshape(-1), axis=2)
-    cache = cache.reshape(2, kv_local, row_count, context, head_dim)
-    queries = query.reshape(row_count, kv_local, group_size, head_dim)
-    scores = jnp.einsum("rkgd,krcd->rkgc", queries, cache[0], preferred_element_type=jnp.float32)
-    scores = scores * head_dim ** (-0.5)
-    valid_keys = jnp.arange(context, dtype=jnp.int32)[None, :] < lengths[:, None]
-    scores = jnp.where(valid_keys[:, None, None, :], scores, -1e30)
-    top_score = jnp.max(scores, axis=-1, keepdims=True)
-    weights = jnp.exp(scores - top_score)
-    probs = (weights / jnp.sum(weights, axis=-1, keepdims=True)).astype(jnp.bfloat16)
-    mixed = jnp.einsum("rkgc,krcd->rkgd", probs, cache[1], preferred_element_type=jnp.float32)
-    attn = mixed.reshape(row_count, kv_local * group_size * head_dim).astype(jnp.bfloat16)
-    part = jnp.einsum("rf,fts->trs", attn, w_out.reshape(-1, RING, SHARE), preferred_element_type=jnp.float32)
-    return experts(
-        part.astype(BF), residual, norm_gain.reshape(1, -1), route_ids, route_weights, w_gate, w_up, w_down
+    return layer(
+        query, kv_pool, page_table.T, lengths, residual, w_out, norm_gain.reshape(-1, 128),
+        route_ids.T, route_weights.T, w_gate, w_up, w_down,
     )
 
 

time: 127 us -> 94.3 us (0.74)
  local copies, waits for them, and re-layouts: 22.3 us -> 1.47 us
  matrix products: 9.72 us -> 0 us
  other arithmetic: 7.78 us -> 0 us
  Pallas kernels: 86.2 us -> 92.6 us
    gather x1 -> x0, local copies, waits for them, and re-layouts: 12 us -> none  [local(): cache = jnp.take(kv_pool, page_table.reshape(-1), axis=2)]
    dot_general x3 -> x0, matrix products: 9.72 us -> none  [the longest x1 5.63 us: local(): jnp.einsum('rf,fts->trs', attn, w_out.reshape(-1, RING, SHARE), preferred...]
    select_n x2 -> x0, other arithmetic: 7.45 us -> none  [local(): cache = jnp.take(kv_pool, page_table.reshape(-1), axis=2)]
    pallas_call x1, Pallas kernels: 86.2 us -> 92.6 us  [layer(): pl.pallas_call(layer_kernel, out_shape=jax.ShapeDtypeStruct((ROWS, SHARE)...]
    slice x1 -> x0, local copies, waits for them, and re-layouts: 5.85 us -> none  [local(): cache[0]]
    unnamed x15 -> x1, local copies, waits for them, and re-layouts: 3.62 us -> 1.47 us
where the time goes in v3:
time: 94.3 us; the launch traced here: 94.1 us
  Pallas kernels  92.6 us (98%)
  local copies, waits for them, and re-layouts  1.47 us (2%)
    pallas_call x1, Pallas kernels, layer(): pl.pallas_call(layer_kernel, out_shape=jax.ShapeDtypeStruct((ROWS, SHARE)...  92.6 us

profile of v3, /device:TPU:1, one launch (start us, length us, event | category | flops | bytes accessed | tf_op | source)
XLA Modules:
  0.0 94.1 jit_solution(13840618483232200614)
XLA Ops:
  0.0 92.6 %shard_map.118 = bf16[32,1024]{1,0:T(8,128)(2,1)} custom-call(bf16[32,1024]{1,0:T(8,128)(2,1)} %query.1, bf16[2,1,256,64,128]{4,3,2,1,0:T(8,128)(2,1)} %kv.1, s32[8,32]{1,0:T(8,128)} %bitcast.5, s32[32]{0:T(128)} %lengths.1, bf16[32,4096]{1,0:T(8,128)(2,1)} %residual.1, bf16[1024,4096]{1,0:T(8,128)(2,1)} %w_out.1, bf16[32,128]{1,0:T(8,128)(2,1)} %bitcast.4, ...), custom_call_target="tpu_custom_call" | custom-call | tf_op jit(solution)/shard_map/pallas_call | solution.py:466
  92.6 1.5 %copy.14 = bf16[32,1024]{1,0:T(8,128)(2,1)} copy(bf16[32,1024]{1,0:T(8,128)(2,1)} %shard_map.118) | data formatting | bytes 131072

commit v4 on v1

v4 whole, which is shorter than its diff:
```python
import functools

import jax
import jax.numpy as jnp
from jax import lax
from jax.experimental import pallas as pl
from jax.experimental.pallas import tpu as pltpu
from jax.sharding import PartitionSpec as P

norm_epsilon = 1e-06
MESH = pl.DeviceIdType.MESH
BF, F32 = jnp.bfloat16, jnp.float32
RING = 4
ROWS = 32
SHARE = 1024
HALF = 16
MANY = 512
GROUP = 8
HEAD = 128
PAGE = 64
PAGES = 256
CONTEXT = 512
HIDDEN = 384
ORDER = (("x", "y", "z"), ("y", "z", "x"), ("z", "x", "y"))
START = (0, 384, 768)
WIDE = (384, 384, 256)
CARRY = 384


def layer_kernel(
    query, kv, pages, lengths, residual, w_out, gain, ids, weights, w_gate, w_up, w_down, out,
    k_in, v_in, w_proj, queries, scores, mixed, part, gains,
    w_in, w_back, rows, acc, act, row_weight, hidden,
    p_in, sq_out, sq_in, sums, away, crossed, l0, l1, l2, f0, f1, f2,
    t0, t1, t2, m0, m1, m2, u0, u1, u2, n0, n1, n2,
    send_sem, recv_sem, load_sem,
):
    rep, y = lax.axis_index("rep"), lax.axis_index("tp")
    x, z, core = rep // 8, (rep // 2) % 4, rep % 2
    at = {"x": x, "y": y, "z": z}
    L, F, T, M, U, N = (l0, l1, l2), (f0, f1, f2), (t0, t1, t2), (m0, m1, m2), (u0, u1, u2), (n0, n1, n2)

    def near(axis, off):
        return lax.rem(at[axis] + off, RING)

    def peer(axis, off):
        c = dict(at)
        c[axis] = near(axis, off)
        return ((c["x"] * RING + c["z"]) * 2 + core, c["y"])

    twin = ((x * RING + z) * 2 + 1 - core, y)

    barrier = pltpu.get_barrier_semaphore()
    others = [peer(a, o) for a in "xyz" for o in (1, 2, 3)] + [twin]
    for other in others:
        pl.semaphore_signal(barrier, inc=1, device_id=other, device_id_type=MESH)

    loads = []
    for i, (src, dst) in enumerate((
        (kv.at[0, 0], k_in),
        (kv.at[1, 0], v_in),
        (w_out, w_proj),
        (w_gate.at[0], w_in.at[:, pl.ds(0, HIDDEN)]),
        (w_up.at[0], w_in.at[:, pl.ds(HIDDEN, HIDDEN)]),
        (w_down.at[0], w_back),
    )):
        load = pltpu.make_async_copy(src, dst, load_sem.at[i])
        if i < 3:
            load.start()
        loads.append(load)

    sends = []

    def send(src, dst, to):
        i = len(sends)
        copy = pltpu.make_async_remote_copy(
            src_ref=src, dst_ref=dst, send_sem=send_sem.at[i], recv_sem=recv_sem.at[i],
            device_id=to, device_id_type=MESH,
        )
        copy.start()
        sends.append(copy)
        return i

    def arrived(i, landing):
        pltpu.make_async_remote_copy(
            src_ref=landing, dst_ref=landing, send_sem=send_sem.at[i], recv_sem=recv_sem.at[i],
            device_id=twin, device_id_type=MESH,
        ).wait_recv()

    for h in range(GROUP):
        queries[h * ROWS : (h + 1) * ROWS, :] = query[:, h * HEAD : (h + 1) * HEAD].astype(F32)
    position = lax.broadcasted_iota(jnp.int32, (GROUP, CONTEXT), 1)

    place = lax.broadcasted_iota(jnp.int32, (128, ROWS), 0)
    spread = jnp.zeros((128, ROWS), F32)
    for k in range(8):
        spread = spread + jnp.where(place % 32 == ids[k : k + 1, :], weights[k : k + 1, :], 0.0)
    top = spread.astype(BF).astype(F32)
    mid = (spread - top).astype(BF).astype(F32)
    low = spread - top - mid
    third = place // 32
    spread = jnp.where(third == 0, top, jnp.where(third == 1, mid, jnp.where(third == 2, low, 0.0)))
    unit = jnp.where(
        lax.broadcasted_iota(jnp.int32, (ROWS, ROWS), 0) == lax.broadcasted_iota(jnp.int32, (ROWS, ROWS), 1), 1.0, 0.0
    ).astype(BF)
    spread = lax.dot_general(unit, spread.astype(BF), (((1,), (1,)), ((), ())), preferred_element_type=F32)
    for h in range(2):
        rows[h, y, x, z, core, :, SHARE : SHARE + 128] = spread[h * HALF : (h + 1) * HALF].astype(BF)
    gains[...] = gain[...].astype(F32)

    def row_pages(store, b):
        return jnp.concatenate([store[pages[j, b]] for j in range(CONTEXT // PAGE)], axis=0)

    def score(b, _):
        q = queries[pl.ds(b, GROUP, stride=ROWS), :].astype(BF)
        s = lax.dot_general(q, row_pages(k_in, b), (((1,), (1,)), ((), ())), preferred_element_type=F32)
        s = jnp.where(position < lengths[b], s * HEAD ** -0.5, -1e30)
        scores[pl.ds(pl.multiple_of(b * GROUP, GROUP), GROUP), :] = s
        return 0

    def mix(b, _):
        p = scores[pl.ds(pl.multiple_of(b * GROUP, GROUP), GROUP), :].astype(BF)
        mixed[pl.ds(b, GROUP, stride=ROWS), :] = jnp.dot(p, row_pages(v_in, b), preferred_element_type=F32)
        return 0

    loads[0].wait()
    lax.fori_loop(0, ROWS, score, 0, unroll=4)
    s = scores[...]
    s = jnp.exp(s - jnp.max(s, axis=1, keepdims=True))
    scores[...] = s / jnp.sum(s, axis=1, keepdims=True)
    loads[1].wait()
    for load in loads[3:]:
        load.start()
    lax.fori_loop(0, ROWS, mix, 0, unroll=4)
    attn = jnp.concatenate([mixed[h * ROWS : (h + 1) * ROWS, :].astype(BF) for h in range(GROUP)], axis=1)
    loads[2].wait()

    def term(t):
        w = w_proj[:, pl.ds(pl.multiple_of(t * SHARE, SHARE), SHARE)]
        return jnp.dot(attn, w, preferred_element_type=F32)

    ids_p, ids_q = {}, {}
    for o in (2, 1, 3):
        value = term(near("y", o)).astype(BF)
        for h in range(2):
            part[h, o - 1] = value[h * HALF : (h + 1) * HALF]
        if o == 2:
            pl.semaphore_wait(barrier, len(others))
        ids_p[0, o] = send(part.at[0, o - 1], p_in.at[0, o - 1], peer("y", o))
    for o in (2, 1, 3):
        ids_p[1, o] = send(part.at[1, o - 1], p_in.at[1, o - 1], peer("y", o))
    col = pl.ds(pl.multiple_of(y * SHARE, SHARE), SHARE)
    hidden[...] = residual[:, col].astype(F32) + term(y)
    own_gain = jnp.concatenate(
        [gains[pl.ds(y * (SHARE // 128) + j, 1), :] for j in range(SHARE // 128)], axis=1
    )

    def add_terms(h):
        r = slice(h * HALF, (h + 1) * HALF)
        total = hidden[r, :]
        for o in (1, 3, 2):
            arrived(ids_p[h, o], p_in.at[h, o - 1])
            total = total + p_in[h, o - 1].astype(F32)
        hidden[r, :] = total
        sq_out[h] = jnp.broadcast_to(jnp.sum(total * total, axis=1, keepdims=True), (HALF, 128))
        for o in (2, 1, 3):
            ids_q[h, o] = send(sq_out.at[h], sq_in.at[h, o - 1], peer("y", o))

    def normalize(h):
        square = sq_out[h]
        for o in (1, 3, 2):
            arrived(ids_q[h, o], sq_in.at[h, o - 1])
            square = square + sq_in[h, o - 1]
        scale = lax.rsqrt(square[:, 0:1] * (1.0 / (RING * SHARE)) + norm_epsilon)
        value = hidden[h * HALF : (h + 1) * HALF, :] * scale * own_gain
        rows[h, y, x, z, core, :, 0:SHARE] = value.astype(BF)

    def box(p, **sel):
        return tuple(pl.ds(*sel.get(a, (0, RING))) for a in "yxz")

    def named(p, i1=None, i2=None, i3=None):
        return {a: i for a, i in zip(ORDER[p], (i1, i2, i3)) if i is not None}

    def block(p, h, c, i1=None, i2=None, i3=None):
        cols = pl.ds(START[p], CARRY)
        return rows.at[(h,) + box(p, **named(p, i1, i2, i3)) + (c, slice(None), cols)]

    own = [tuple(at[a] for a in ORDER[p]) for p in range(3)]
    ids_g = {}

    def ag1(h):
        for p in range(3):
            q1, q2, q3 = own[p]
            ref = block(p, h, core, (q1, 1), (q2, 1), (q3, 1))
            for o in (1, 3, 2):
                ids_g[1, p, h, o] = send(ref, ref, peer(ORDER[p][0], o))

    def ag2(h):
        for p in range(3):
            q1, q2, q3 = own[p]
            for o in (1, 3, 2):
                arrived(ids_g[1, p, h, o], block(p, h, core, (near(ORDER[p][0], 4 - o), 1), (q2, 1), (q3, 1)))
            ref = block(p, h, core, None, (q2, 1), (q3, 1))
            for o in (1, 3, 2):
                ids_g[2, p, h, o] = send(ref, ref, peer(ORDER[p][1], o))

    def to_twin(p, h, d):
        ref = block(p, h, core, None, None, (near(ORDER[p][2], (4 - d) % 4), 1))
        ids_g["twin", p, h, d] = send(ref, ref, twin)

    def ag3(h):
        for p in range(3):
            q1, q2, q3 = own[p]
            for o in (1, 3, 2):
                arrived(ids_g[2, p, h, o], block(p, h, core, None, (near(ORDER[p][1], 4 - o), 1), (q3, 1)))
            for turn in range(2):
                for k, o in enumerate((1, 3)):
                    ref = block(p, h, core, (2 * ((k + turn) % 2), 2), None, (q3, 1))
                    ids_g[3, p, h, o, turn] = send(ref, ref, peer(ORDER[p][2], o))
        for p in range(3):
            to_twin(p, h, 0)

    def ag4(h):
        for p in range(3):
            for k, o in enumerate((1, 3)):
                ref = block(p, h, core, (2 * k, 2), None, (near(ORDER[p][2], 4 - o), 1))
                arrived(ids_g[3, p, h, o, 0], ref)
                ids_g[4, p, h, o] = send(ref, ref, peer(ORDER[p][2], o))

    def ag5(h):
        for p in range(3):
            for k, o in enumerate((1, 3)):
                arrived(ids_g[3, p, h, o, 1], block(p, h, core, (2 - 2 * k, 2), None, (near(ORDER[p][2], 4 - o), 1)))
                to_twin(p, h, o)

    def ag6(h):
        for p in range(3):
            for k, o in enumerate((1, 3)):
                arrived(ids_g[4, p, h, o], block(p, h, core, (2 * k, 2), None, (near(ORDER[p][2], 2), 1)))
            to_twin(p, h, 2)

    def ag7(h):
        for d in (0, 1, 3, 2):
            for p in range(3):
                ref = block(p, h, 1 - core, None, None, (near(ORDER[p][2], (4 - d) % 4), 1))
                arrived(ids_g["twin", p, h, d], ref)

    pick = lax.broadcasted_iota(jnp.int32, (128, 128), 0)
    pick = jnp.where((pick % 32 == rep) & (pick < 96), 1.0, 0.0).astype(BF)

    def enter(h, *steps):
        for t in steps:
            value = rows[h, t, :, :, :, :, 0:SHARE].reshape(MANY, SHARE)
            value = jnp.dot(value, w_in[t * SHARE : (t + 1) * SHARE, :], preferred_element_type=F32)
            if t == 0:
                acc[...] = value
            else:
                acc[...] += value

    def units(h):
        table = rows[h, y, :, :, :, :, SHARE : SHARE + 128].reshape(MANY, 128)
        weight = jnp.dot(table, pick, preferred_element_type=F32)
        row_weight[...] = weight.reshape(MANY // 32, 2, HALF, 128)
        g = acc[:, 0:HIDDEN]
        u = acc[:, HIDDEN : 2 * HIDDEN]
        act[...] = (g / (1.0 + jnp.exp(-g)) * u).astype(BF).reshape(MANY // 32, 2, HALF, HIDDEN)

    ids_b = {}

    def terms(mine, t):
        w = w_back[:, pl.ds(pl.multiple_of(t * SHARE, SHARE), SHARE)]
        value = jnp.dot(act[:, mine].reshape(MANY // 2, HIDDEN), w, preferred_element_type=F32)
        rw = row_weight[:, mine].reshape(MANY // 2, 128)
        value = jnp.concatenate([value[:, j * 128 : (j + 1) * 128] * rw for j in range(SHARE // 128)], axis=1)
        return value.reshape(RING, RING, HALF, SHARE)

    def leave_twin(h, o):
        t = near("y", o)
        away[h, t] = terms(1 - core, t).astype(BF)
        ids_b["twin", h, o] = send(away.at[h, t], crossed.at[h, t], twin)

    def leave_own(h, o):
        t = near("y", o)
        value = terms(core, t)
        arrived(ids_b["twin", h, o], crossed.at[h, t])
        sums[h, t] = (value + crossed[h, t].astype(F32)).astype(BF)

    def term_of(p, h, i1=None, i2=None, i3=None):
        cols = pl.ds(START[p], WIDE[p])
        return sums.at[(h,) + box(p, **named(p, i1, i2, i3)) + (slice(None), cols)]

    def part_of(ref, lead, p, i1=None, i2=None):
        return ref[p].at[lead + box(p, **named(p, i1, i2, (0, 1)))]

    def rs1(h, pieces):
        for p in pieces:
            axis = ORDER[p][2]
            far = (near(axis, 2), 1)
            for k, o in enumerate((1, 3)):
                ids_b[1, p, h, o] = send(term_of(p, h, (2 * k, 2), None, far), L[p].at[h, k], peer(axis, o))
            for k, o in enumerate((1, 3)):
                ids_b[2, p, h, o, 0] = send(
                    term_of(p, h, (2 - 2 * k, 2), None, (near(axis, o), 1)),
                    part_of(F, (h, k), p, (2 - 2 * k, 2)), peer(axis, o),
                )

    def rs2(h):
        for p in range(3):
            axis = ORDER[p][2]
            for k, o in enumerate((1, 3)):
                arrived(ids_b[1, p, h, o], L[p].at[h, k])
                ref = term_of(p, h, (2 * k, 2), None, (near(axis, o), 1))
                ref[...] = ref[...] + L[p][h, k]
                ids_b[2, p, h, o, 1] = send(ref, part_of(F, (h, k), p, (2 * k, 2)), peer(axis, o))

    def rs3(h):
        for p in range(3):
            for k, o in enumerate((1, 3)):
                arrived(ids_b[2, p, h, o, 0], part_of(F, (h, k), p, (2 - 2 * k, 2)))
                arrived(ids_b[2, p, h, o, 1], part_of(F, (h, k), p, (2 * k, 2)))
            value = term_of(p, h, None, None, (own[p][2], 1))[...].astype(F32)
            T[p][h] = (value + F[p][h, 0].astype(F32) + F[p][h, 1].astype(F32)).astype(BF)
            axis = ORDER[p][1]
            for o in (2, 1, 3):
                ref = part_of(T, (h,), p, None, (near(axis, o), 1))
                ids_b[3, p, h, o] = send(ref, M[p].at[h, o - 1], peer(axis, o))

    def rs4(h):
        for p in range(3):
            value = part_of(T, (h,), p, None, (own[p][1], 1))[...].astype(F32)
            for o in (1, 3, 2):
                arrived(ids_b[3, p, h, o], M[p].at[h, o - 1])
                value = value + M[p][h, o - 1].astype(F32)
            U[p][h] = value.astype(BF).reshape(RING, HALF, WIDE[p])
            for o in (2, 1, 3):
                ids_b[4, p, h, o] = send(U[p].at[h, near(ORDER[p][0], o)], N[p].at[h, o - 1], peer(ORDER[p][0], o))

    def rs5(h):
        r = slice(h * HALF, (h + 1) * HALF)
        for p in range(3):
            value = U[p][h, own[p][0]].astype(F32)
            for o in (1, 3, 2):
                arrived(ids_b[4, p, h, o], N[p].at[h, o - 1])
                value = value + N[p][h, o - 1].astype(F32)
            c = slice(START[p], START[p] + WIDE[p])
            out[r, c] = (hidden[r, c] + value).astype(BF)

    add_terms(0)
    add_terms(1)
    normalize(0)
    ag1(0)
    normalize(1)
    ag1(1)
    ag2(0)
    ag3(0)
    ag2(1)
    ag4(0)
    ag3(1)
    ag5(0)
    ag6(0)
    for load in loads[3:]:
        load.wait()
    ag7(0)
    enter(0, 0)
    ag4(1)
    enter(0, 1, 2)
    ag5(1)
    enter(0, 3)
    units(0)
    for o in (2, 1, 3, 0):
        leave_twin(0, o)
    ag6(1)
    for o in (2, 1, 3):
        leave_own(0, o)
    rs1(0, (2,))
    leave_own(0, 0)
    rs1(0, (0, 1))
    ag7(1)
    enter(1, 0, 1)
    rs2(0)
    enter(1, 2, 3)
    units(1)
    for o in (2, 1, 3, 0):
        leave_twin(1, o)
    rs3(0)
    for o in (2, 1, 3):
        leave_own(1, o)
    rs1(1, (2,))
    leave_own(1, 0)
    rs1(1, (0, 1))
    rs4(0)
    rs2(1)
    rs5(0)
    rs3(1)
    rs4(1)
    rs5(1)

    for copy in sends:
        copy.wait_send()


SEMS = 12 + 2 * 3 * (3 + 3 + 4 + 2 + 4) + 2 * (4 + 3 * (2 + 4 + 3 + 3))


def layer(*operands):
    smem = pl.BlockSpec(memory_space=pltpu.SMEM)
    vmem = pl.BlockSpec(memory_space=pltpu.VMEM)
    hbm = pl.BlockSpec(memory_space=pl.ANY)
    V = pltpu.VMEM
    R = RING
    scratch = [
        V((PAGES, PAGE, HEAD), BF),
        V((PAGES, PAGE, HEAD), BF),
        V((SHARE, R * SHARE), BF),
        V((GROUP * ROWS, HEAD), F32),
        V((GROUP * ROWS, CONTEXT), F32),
        V((GROUP * ROWS, HEAD), F32),
        V((2, 3, HALF, SHARE), BF),
        V((32, 128), F32),
        V((R * SHARE, 2 * HIDDEN), BF),
        V((HIDDEN, R * SHARE), BF),
        V((2, R, R, R, 2, HALF, SHARE + 128), BF),
        V((MANY, 2 * HIDDEN), F32),
        V((MANY // 32, 2, HALF, HIDDEN), BF),
        V((MANY // 32, 2, HALF, 128), F32),
        V((ROWS, SHARE), F32),
        V((2, 3, HALF, SHARE), BF),
        V((2, HALF, 128), F32),
        V((2, 3, HALF, 128), F32),
        V((2, R, R, R, HALF, SHARE), BF),
        V((2, R, R, R, HALF, SHARE), BF),
        V((2, R, R, R, HALF, SHARE), BF),
    ]

    def sizes(p, *cut):
        cut = dict(zip(ORDER[p][::-1], cut))
        return tuple(cut.get(a, R) for a in "yxz") + (HALF, WIDE[p])

    scratch += [V((2, 2) + sizes(p, 1, R, 2), BF) for p in range(3)]
    scratch += [V((2, 2) + sizes(p, 1), BF) for p in range(3)]
    scratch += [V((2,) + sizes(p, 1), BF) for p in range(3)]
    scratch += [V((2, 3) + sizes(p, 1, 1), BF) for p in range(3)]
    scratch += [V((2, R, HALF, w), BF) for w in WIDE]
    scratch += [V((2, 3, HALF, w), BF) for w in WIDE]
    scratch += [pltpu.SemaphoreType.DMA((SEMS,)), pltpu.SemaphoreType.DMA((SEMS,)), pltpu.SemaphoreType.DMA((6,))]
    return pl.pallas_call(
        layer_kernel,
        out_shape=jax.ShapeDtypeStruct((ROWS, SHARE), BF),
        in_specs=[vmem, hbm, smem, smem, vmem, hbm] + [vmem] * 3 + [hbm] * 3,
        out_specs=vmem,
        scratch_shapes=scratch,
        compiler_params=pltpu.CompilerParams(
            collective_id=0, has_side_effects=True, vmem_limit_bytes=61 * 1024 * 1024
        ),
    )(*operands)


def local(
    query, kv_pool, page_table, lengths, residual, w_out, norm_gain,
    route_ids, route_weights, w_gate, w_up, w_down,
):
    return layer(
        query, kv_pool, page_table.T, lengths, residual, w_out, norm_gain.reshape(-1, 128),
        route_ids.T, route_weights.T, w_gate, w_up, w_down,
    )


def solution(mesh):
    in_specs = (
        P("rep", "tp"),
        P(None, "tp", "rep", None, None),
        P("rep", None),
        P("rep"),
        P("rep", None),
        P("tp", None),
        P(),
        P("rep", None),
        P("rep", None),
        P("rep", None, "tp"),
        P("rep", None, "tp"),
        P("rep", "tp", None),
    )
    out_specs = P("rep", "tp")
    return jax.shard_map(local, mesh=mesh, in_specs=in_specs, out_specs=out_specs, check_vma=False)
```

time: 335 us -> 89 us (0.27)
  waiting for transfers between devices: 209 us -> 0 us
  Pallas kernels: 0 us -> 87.3 us
  blocking collectives: 49 us -> 0 us
  matrix products: 29.4 us -> 0 us
  local copies, waits for them, and re-layouts: 20.3 us -> 1.47 us
  between operations: 13.3 us -> 0.01 us
  other arithmetic: 12.1 us -> 0 us
    reduce_scatter x3 -> x0, waiting for transfers between devices: 183 us -> none  [the longest x1 80.5 us: local(): moe = lax.psum_scatter(moe, 'rep', scatter_dimension=0, tiled=True)]
    pallas_call x0 -> x1, Pallas kernels: none -> 87.3 us  [layer(): pl.pallas_call(layer_kernel, out_shape=jax.ShapeDtypeStruct((ROWS, SHARE)...]
    all_gather x2 -> x0, blocking collectives: 42.4 us -> none  [the longest x1 32.3 us: local(): spread_all = lax.all_gather(spread, 'rep', axis=0, tiled=True)]
    dot_general x6 -> x0, matrix products: 29.4 us -> none  [the longest x1 7.97 us: local(): gate = jnp.dot(rows, w_gate[0], preferred_element_type=jnp.float32)]
    all_gather x1 -> x0, waiting for transfers between devices: 26.8 us -> none  [local(): rows = lax.all_gather(rows, 'rep', axis=0, tiled=True)]
    gather x1 -> x0, local copies, waits for them, and re-layouts: 12 us -> none  [local(): cache = jnp.take(kv_pool, page_table.reshape(-1), axis=2)]
    select_n x2 -> x0, other arithmetic: 7.45 us -> none  [local(): cache = jnp.take(kv_pool, page_table.reshape(-1), axis=2)]
    psum x1 -> x0, blocking collectives: 6.53 us -> none  [local(): lax.psum(jnp.sum(hidden * hidden, axis=-1, keepdims=True), 'tp')]
  transfers between devices with their start and end apart: 4 -> 0, of which waited for: 4 -> 0; matrix products, arithmetic and copies ran while one was open for 0% -> 0% of each run, Pallas kernels for 0% -> 0%
where the time goes in v4:
time: 89 us; the launch traced here: 88.8 us
  Pallas kernels  87.3 us (98%)
  local copies, waits for them, and re-layouts  1.47 us (2%)
    pallas_call x1, Pallas kernels, layer(): pl.pallas_call(layer_kernel, out_shape=jax.ShapeDtypeStruct((ROWS, SHARE)...  87.3 us

profile of v4, /device:TPU:1, one launch (start us, length us, event | category | flops | bytes accessed | tf_op | source)
XLA Modules:
  0.0 88.8 jit_solution(17226576370017289024)
XLA Ops:
  0.0 87.3 %shard_map.118 = bf16[32,1024]{1,0:T(8,128)(2,1)} custom-call(bf16[32,1024]{1,0:T(8,128)(2,1)} %query.1, bf16[2,1,256,64,128]{4,3,2,1,0:T(8,128)(2,1)} %kv.1, s32[8,32]{1,0:T(8,128)} %bitcast.5, s32[32]{0:T(128)} %lengths.1, bf16[32,4096]{1,0:T(8,128)(2,1)} %residual.1, bf16[1024,4096]{1,0:T(8,128)(2,1)} %w_out.1, bf16[32,128]{1,0:T(8,128)(2,1)} %bitcast.4, ...), custom_call_target="tpu_custom_call" | custom-call | tf_op jit(solution)/shard_map/pallas_call | solution.py:446
  87.3 1.5 %copy.14 = bf16[32,1024]{1,0:T(8,128)(2,1)} copy(bf16[32,1024]{1,0:T(8,128)(2,1)} %shard_map.118) | data formatting | bytes 131072

commit v5 on v4

--- a/solution.py
+++ b/solution.py
@@ -13,6 +13,7 @@
 RING = 4
 ROWS = 32
 SHARE = 1024
+EARLY = 16
 HALF = 16
 MANY = 512
 GROUP = 8
@@ -57,15 +58,15 @@
 
     loads = []
     for i, (src, dst) in enumerate((
-        (kv.at[0, 0], k_in),
-        (kv.at[1, 0], v_in),
-        (w_out, w_proj),
+        *[(kv.at[0, 0, pl.ds(i * 64, 64)], k_in.at[pl.ds(i * 64, 64)]) for i in range(4)],
+        *[(kv.at[1, 0, pl.ds(i * 64, 64)], v_in.at[pl.ds(i * 64, 64)]) for i in range(4)],
+        *[(w_out.at[pl.ds(i * 128, 128)], w_proj.at[pl.ds(i * 128, 128)]) for i in range(8)],
         (w_gate.at[0], w_in.at[:, pl.ds(0, HIDDEN)]),
         (w_up.at[0], w_in.at[:, pl.ds(HIDDEN, HIDDEN)]),
         (w_down.at[0], w_back),
     )):
         load = pltpu.make_async_copy(src, dst, load_sem.at[i])
-        if i < 3:
+        if i < EARLY:
             load.start()
         loads.append(load)
 
@@ -123,17 +124,20 @@
         mixed[pl.ds(b, GROUP, stride=ROWS), :] = jnp.dot(p, row_pages(v_in, b), preferred_element_type=F32)
         return 0
 
-    loads[0].wait()
+    for load in loads[0:4]:
+        load.wait()
     lax.fori_loop(0, ROWS, score, 0, unroll=4)
     s = scores[...]
     s = jnp.exp(s - jnp.max(s, axis=1, keepdims=True))
     scores[...] = s / jnp.sum(s, axis=1, keepdims=True)
-    loads[1].wait()
-    for load in loads[3:]:
+    for load in loads[4:8]:
+        load.wait()
+    for load in loads[EARLY:]:
         load.start()
     lax.fori_loop(0, ROWS, mix, 0, unroll=4)
     attn = jnp.concatenate([mixed[h * ROWS : (h + 1) * ROWS, :].astype(BF) for h in range(GROUP)], axis=1)
-    loads[2].wait()
+    for load in loads[8:EARLY]:
+        load.wait()
 
     def term(t):
         w = w_proj[:, pl.ds(pl.multiple_of(t * SHARE, SHARE), SHARE)]
@@ -352,13 +356,13 @@
     normalize(1)
     ag1(1)
     ag2(0)
+    ag2(1)
     ag3(0)
-    ag2(1)
+    ag3(1)
     ag4(0)
-    ag3(1)
     ag5(0)
     ag6(0)
-    for load in loads[3:]:
+    for load in loads[EARLY:]:
         load.wait()
     ag7(0)
     enter(0, 0)
@@ -442,7 +446,7 @@
     scratch += [V((2, 3) + sizes(p, 1, 1), BF) for p in range(3)]
     scratch += [V((2, R, HALF, w), BF) for w in WIDE]
     scratch += [V((2, 3, HALF, w), BF) for w in WIDE]
-    scratch += [pltpu.SemaphoreType.DMA((SEMS,)), pltpu.SemaphoreType.DMA((SEMS,)), pltpu.SemaphoreType.DMA((6,))]
+    scratch += [pltpu.SemaphoreType.DMA((SEMS,)), pltpu.SemaphoreType.DMA((SEMS,)), pltpu.SemaphoreType.DMA((EARLY + 3,))]
     return pl.pallas_call(
         layer_kernel,
         out_shape=jax.ShapeDtypeStruct((ROWS, SHARE), BF),

time: 89 us -> 87.9 us (0.988)
  Pallas kernels: 87.3 us -> 86.1 us
    pallas_call x1, Pallas kernels: 87.3 us -> 86.1 us  [layer(): pl.pallas_call(layer_kernel, out_shape=jax.ShapeDtypeStruct((ROWS, SHARE)...]
where the time goes in v5:
time: 87.9 us; the launch traced here: 87.6 us
  Pallas kernels  86.1 us (98%)
  local copies, waits for them, and re-layouts  1.47 us (2%)
    pallas_call x1, Pallas kernels, layer(): pl.pallas_call(layer_kernel, out_shape=jax.ShapeDtypeStruct((ROWS, SHARE)...  86.1 us

profile of v5, /device:TPU:1, one launch (start us, length us, event | category | flops | bytes accessed | tf_op | source)
XLA Modules:
  0.0 87.6 jit_solution(6274901810379117263)
XLA Ops:
  0.0 86.1 %shard_map.118 = bf16[32,1024]{1,0:T(8,128)(2,1)} custom-call(bf16[32,1024]{1,0:T(8,128)(2,1)} %query.1, bf16[2,1,256,64,128]{4,3,2,1,0:T(8,128)(2,1)} %kv.1, s32[8,32]{1,0:T(8,128)} %bitcast.5, s32[32]{0:T(128)} %lengths.1, bf16[32,4096]{1,0:T(8,128)(2,1)} %residual.1, bf16[1024,4096]{1,0:T(8,128)(2,1)} %w_out.1, bf16[32,128]{1,0:T(8,128)(2,1)} %bitcast.4, ...), custom_call_target="tpu_custom_call" | custom-call | tf_op jit(solution)/shard_map/pallas_call | solution.py:450
  86.1 1.5 %copy.14 = bf16[32,1024]{1,0:T(8,128)(2,1)} copy(bf16[32,1024]{1,0:T(8,128)(2,1)} %shard_map.118) | data formatting | bytes 131072
